TPU v7x, 512 devices: a whole 4x8x8 slice. The times are simulated.
512 devices in a mesh: gx: 16 (over x, y_hi), gy: 32 (over z, y_lo, core).
Axes of the slice: x: 4, y: 8 (y_hi: 4, y_lo: 2; y = y_hi * 2 + y_lo), z: 8, core: 2. Of those that a mesh axis runs over, the one named last changes fastest.
Arguments:
- charge: float32 [16, 32, 256], P('gx', 'gy'), may hold values from -9 to 9
- fraction: float32 [3, 16, 32, 256], P(None, 'gx', 'gy'), may hold values from 0 to 1
- base_cell: int32 [16, 32, 256], P('gx', 'gy'), may hold values from 0 to 2047, as said below
- live_slot: int32 [16, 32, 256], P('gx', 'gy'), may hold values 0 or 1
- force_cot: float32 [3, 16, 32, 256], P(None, 'gx', 'gy'), may hold values from -6 to 6
- potential_cot: float32 [16, 32, 256], P('gx', 'gy'), may hold values from -6 to 6
Outputs:
- forces: float32 [3, 16, 32, 256], P(None, 'gx', 'gy')
- potential: float32 [16, 32, 256], P('gx', 'gy')
- charge_grad: float32 [16, 32, 256], P('gx', 'gy')
Inputs may be any that keep to these rules, and one draw needn't show every extreme that they name: `base_cell`: x * 8 * 16 + y * 16 + z for the atom's base cell counted inside its domain, z inside the block of its slot; slot s belongs to block s // 16.
All inputs are finite; a program needn't handle non-finite values. No bound on the sum of `live_slot` on one device may be relied on, other than what follows from the above.
Results may differ from a plain program's by a relative error of at most 0.0003.
Values sent between devices are 32-bit elements; how exact they have to be, the bound alone decides.
No kernel may reach another device: no remote copies, remote signals or barrier semaphores. Data moves between devices by JAX's collectives and lax.ppermute only.
A program may use at most 64 MiB of HBM per device.

v0:
```python
import math

import jax
import jax.numpy as jnp
import ml_dtypes
import numpy as np
from jax import lax
from jax.experimental import pallas as pl
from jax.experimental.pallas import tpu as pltpu
from jax.sharding import PartitionSpec as P

K = 256
CX = 16
CY = 8
EX = CX + 3
EY = CY + 3
N_GX = 16
N_GY = 32
ATOMS = 256
DEVICES = N_GX * N_GY
LANES = 128

EWALD_SPLIT = 0.8


def cas_table(left, right):
    angles = 2.0 * math.pi / K * (left[:, None] * right[None, :] % K)
    return np.cos(angles) + np.sin(angles)


def split_table(table):
    high = table.astype(np.float32).astype(ml_dtypes.bfloat16)
    low = (table - high.astype(np.float64)).astype(np.float32).astype(ml_dtypes.bfloat16)
    return np.stack([high, low])


def extended_coordinates():
    gx, a = np.meshgrid(np.arange(N_GX), np.arange(EX), indexing="ij")
    ext_x = (gx * CX + a - 1).reshape(-1) % K
    b, gy = np.meshgrid(np.arange(EY), np.arange(N_GY), indexing="ij")
    ext_y = (gy * CY + b - 1).reshape(-1) % K
    return ext_x, ext_y


def influence_factors():
    freq = np.arange(K)
    nearest = np.minimum(freq, K - freq).astype(np.float64)
    damping = math.pi * math.pi / (EWALD_SPLIT * EWALD_SPLIT * K * K)
    cosine = np.cos(2.0 * math.pi / K * freq)
    factor = np.exp(-damping * nearest * nearest) * 9.0 / (2.0 + cosine) ** 2
    return factor.astype(np.float32), (nearest * nearest).astype(np.float32)


def split(value):
    high = value.astype(jnp.bfloat16)
    low = (value - high.astype(jnp.float32)).astype(jnp.bfloat16)
    return high, low


def product(left, right, dims=((1,), (0,))):
    def one(a, b):
        return lax.dot_general(a, b, (dims, ((), ())), preferred_element_type=jnp.float32)

    return one(left[0], right[0]) + (one(left[0], right[1]) + one(left[1], right[0]))


def spline_terms(fraction):
    square = fraction * fraction
    cubic_part = square * fraction
    remain = 1.0 - fraction
    weights = (
        remain * remain * remain * (1.0 / 6.0),
        (3.0 * cubic_part - 6.0 * square + 4.0) * (1.0 / 6.0),
        (-3.0 * cubic_part + 3.0 * square + 3.0 * fraction + 1.0) * (1.0 / 6.0),
        cubic_part * (1.0 / 6.0),
    )
    slopes = (
        -0.5 * remain * remain,
        (3.0 * square - 4.0 * fraction) * 0.5,
        (-3.0 * square + 2.0 * fraction + 1.0) * 0.5,
        0.5 * square,
    )
    return weights, slopes


def banded(first, terms, rows, wrap):
    place = lax.broadcasted_iota(jnp.int32, (rows, ATOMS), 0) - first
    if wrap:
        place = jnp.bitwise_and(place, rows - 1)
    hits = [place == offset for offset in range(4)]

    def table(values):
        out = jnp.zeros((rows, ATOMS), jnp.float32)
        for hit, value in zip(hits, values):
            out = jnp.where(hit, jnp.broadcast_to(value, (rows, ATOMS)), out)
        return out

    return [table(values) for values in terms]


def domain_tables(cells, fraction_ref):
    wx, dx = banded(jnp.right_shift(cells, 7), spline_terms(fraction_ref[0, 0]), 24, False)
    cell_y = jnp.bitwise_and(jnp.right_shift(cells, 4), CY - 1)
    wy, dy = banded(cell_y, spline_terms(fraction_ref[1, 0]), 16, False)
    return wx, dx, wy, dy


def spread_kernel(
    charge, fraction, base_cell, live_slot, force_cot, potential_cot, hartley,
    send, spectral, table_a, table_b, table_c,
):
    live = live_slot[0].astype(jnp.float32)
    live_charge = charge[0] * live
    cells = base_cell[0]
    slot = lax.broadcasted_iota(jnp.int32, (1, ATOMS), 1)
    base_z = jnp.bitwise_and(slot, -16) + jnp.bitwise_and(cells, 15)
    wz, dz = banded(base_z - 1, spline_terms(fraction[2, 0]), K, True)
    hart = (hartley[0], hartley[1])
    zw = split(product(hart, split(wz)))
    zd = split(product(hart, split(dz)))
    spectral[0] = zw[0]
    spectral[1] = zw[1]
    spectral[2] = zd[0]
    spectral[3] = zd[1]

    wx, dx, wy, dy = domain_tables(cells, fraction)
    along_x = -live_charge * force_cot[0, 0]
    along_y = -live_charge * force_cot[1, 0]
    along_z = -live_charge * force_cot[2, 0]
    direct = live * potential_cot[0]
    tail = jnp.zeros((48, ATOMS), jnp.float32)
    for table in (table_a, table_b, table_c):
        table[208:256, :] = tail
    for b in range(EY):
        wyb = wy[b : b + 1]
        dyb = dy[b : b + 1]
        rows = pl.ds(b * EX, 24)
        table_a[rows, :] = wx * (live_charge * wyb)
        table_b[rows, :] = dx * (along_x * wyb) + wx * (along_y * dyb + direct * wyb)
        table_c[rows, :] = wx * (along_z * wyb)
    nt = ((1,), (1,))
    first = product(zw, split(table_a[...]), nt)
    second = product(zw, split(table_b[...]), nt) + product(zd, split(table_c[...]), nt)
    for field, value in enumerate((first, second)):
        for half in range(2):
            send[pl.ds(field * 2 * K + half, K, stride=2), :] = value[
                :, half * LANES : (half + 1) * LANES
            ]


def plane_kernel(
    received, hx, hxt, hy, hyt, row_terms, column_terms, scalar_terms, send, plane, blocks
):
    device = lax.axis_index("gx") * N_GY + lax.axis_index("gy")
    freq_z = lax.rem(device, K)
    plane[:, 256:384] = jnp.zeros((EY * N_GY, LANES), jnp.float32)
    for gx in range(N_GX):
        rows = jnp.concatenate(
            [received[pl.ds(gx * 2 * N_GY + half, N_GY, stride=2), :] for half in range(2)], axis=1
        )
        for b in range(EY):
            plane[b * N_GY : (b + 1) * N_GY, gx * EX : (gx + 1) * EX] = rows[
                :, b * EX : (b + 1) * EX
            ]
    mesh_plane = plane[:, : N_GX * EX]
    half_way = product(split(mesh_plane), (hx[0], hx[1]))
    spectrum = product((hyt[0], hyt[1]), split(half_way))
    total_sq = (column_terms[:, 1:2] + row_terms[1:2, :]) + scalar_terms[1, freq_z]
    factor = column_terms[:, 0:1] * (row_terms[0:1, :] * (scalar_terms[0, freq_z] / (math.pi * K)))
    kernel = jnp.where(total_sq > 0.0, factor / jnp.maximum(total_sq, 1.0), 0.0)
    half_way = product((hy[0], hy[1]), split(spectrum * kernel))
    plane[:, : N_GX * EX] = product(split(half_way), (hxt[0], hxt[1]))
    blocks[:, LANES:] = jnp.zeros((DEVICES, LANES), jnp.float32)
    for b in range(EY):
        rows = plane[b * N_GY : (b + 1) * N_GY, :]
        for gx in range(N_GX):
            blocks[gx * N_GY : (gx + 1) * N_GY, b * EX : (b + 1) * EX] = rows[
                :, gx * EX : (gx + 1) * EX
            ]
    for half in range(2):
        send[pl.ds(half, DEVICES, stride=2), :] = blocks[:, half * LANES : (half + 1) * LANES]


def sample_kernel(
    received, spectral, charge, fraction, base_cell, live_slot, force_cot,
    forces, potential, charge_grad, sample_a, sample_b, sample_c,
):
    def field(index):
        halves = [received[pl.ds(index * 2 * K + half, K, stride=2), :] for half in range(2)]
        return split(jnp.concatenate(halves, axis=1).T)

    zw = (spectral[0], spectral[1])
    zd = (spectral[2], spectral[3])
    first = field(0)
    sample_a[...] = product(first, zw)
    sample_b[...] = product(first, zd)
    sample_c[...] = product(field(1), zw)
    live = live_slot[0].astype(jnp.float32)
    live_charge = charge[0] * live
    wx, dx, wy, dy = domain_tables(base_cell[0], fraction)
    sums = [jnp.zeros((24, ATOMS), jnp.float32) for _ in range(5)]
    for b in range(EY):
        wyb = wy[b : b + 1]
        dyb = dy[b : b + 1]
        rows = pl.ds(b * EX, 24)
        plain = sample_a[rows, :]
        plain_x = wx * plain
        sums[0] = sums[0] + plain_x * wyb
        sums[1] = sums[1] + (dx * plain) * wyb
        sums[2] = sums[2] + plain_x * dyb
        sums[3] = sums[3] + (wx * sample_b[rows, :]) * wyb
        sums[4] = sums[4] + (wx * sample_c[rows, :]) * wyb
    mesh_value, grad_x, grad_y, grad_z, response = [
        jnp.sum(value, axis=0, keepdims=True) for value in sums
    ]
    forces[0, 0] = -live_charge * grad_x
    forces[1, 0] = -live_charge * grad_y
    forces[2, 0] = -live_charge * grad_z
    potential[0] = live * mesh_value
    charge_grad[0] = live * (
        response
        - force_cot[0, 0] * grad_x
        - force_cot[1, 0] * grad_y
        - force_cot[2, 0] * grad_z
    )


def exchange(blocks):
    swapped = lax.all_to_all(
        blocks.reshape(DEVICES, 2, LANES), ("gx", "gy"), split_axis=0, concat_axis=0, tiled=True
    )
    return swapped.reshape(2 * DEVICES, LANES)


def on_device(charge, fraction, base_cell, live_slot, force_cot, potential_cot):
    ext_x, ext_y = extended_coordinates()
    freq = np.arange(K)
    factor, squares = influence_factors()
    terms = np.stack([factor, squares])
    hx = cas_table(ext_x, freq)
    hy = cas_table(ext_y, freq)
    params = pltpu.CompilerParams(vmem_limit_bytes=48 * 1024 * 1024)
    vmem = pl.BlockSpec(memory_space=pltpu.VMEM)
    smem = pl.BlockSpec(memory_space=pltpu.SMEM)
    f32 = jnp.float32
    table = pltpu.VMEM((K, ATOMS), f32)
    message = jax.ShapeDtypeStruct((2 * DEVICES, LANES), f32)

    sent, spectral = pl.pallas_call(
        spread_kernel,
        out_shape=(message, jax.ShapeDtypeStruct((4, K, ATOMS), jnp.bfloat16)),
        in_specs=[vmem] * 7,
        out_specs=(vmem, vmem),
        scratch_shapes=[table, table, table],
        compiler_params=params,
        name="spread",
    )(
        charge, fraction, base_cell, live_slot, force_cot, potential_cot,
        jnp.asarray(split_table(cas_table(freq, freq))),
    )
    received = exchange(sent)
    solved = pl.pallas_call(
        plane_kernel,
        out_shape=message,
        in_specs=[vmem] * 7 + [smem],
        out_specs=vmem,
        scratch_shapes=[pltpu.VMEM((EY * N_GY, 384), f32), pltpu.VMEM((DEVICES, 2 * LANES), f32)],
        compiler_params=params,
        name="plane",
    )(
        received,
        jnp.asarray(split_table(hx)),
        jnp.asarray(split_table(hx.T)),
        jnp.asarray(split_table(hy)),
        jnp.asarray(split_table(hy.T)),
        jnp.asarray(terms),
        jnp.asarray(terms.T),
        jnp.asarray(terms),
    )
    returned = exchange(solved)
    return pl.pallas_call(
        sample_kernel,
        out_shape=(
            jax.ShapeDtypeStruct((3, 1, 1, ATOMS), f32),
            jax.ShapeDtypeStruct((1, 1, ATOMS), f32),
            jax.ShapeDtypeStruct((1, 1, ATOMS), f32),
        ),
        in_specs=[vmem] * 7,
        out_specs=(vmem, vmem, vmem),
        scratch_shapes=[table, table, table],
        compiler_params=params,
        name="sample",
    )(returned, spectral, charge, fraction, base_cell, live_slot, force_cot)


def solution(mesh):
    return jax.shard_map(
        on_device,
        mesh=mesh,
        in_specs=(
            P("gx", "gy", None),
            P(None, "gx", "gy", None),
            P("gx", "gy", None),
            P("gx", "gy", None),
            P(None, "gx", "gy", None),
            P("gx", "gy", None),
        ),
        out_specs=(P(None, "gx", "gy", None), P("gx", "gy", None), P("gx", "gy", None)),
        check_vma=False,
    )
```

profile of v0, /device:TPU:1, one launch (start us, length us, event | category | flops | bytes accessed | tf_op | source)
XLA Modules:
  0.0 88.6 jit_solution(12904363863684087838)
XLA Ops:
  0.6 0.0 copy-start.4
  0.6 0.9 %copy-done.4 = bf16[2,256,256]{2,1,0:T(8,128)(2,1)S(1)} copy-done((bf16[2,256,256]{2,1,0:T(8,128)(2,1)S(1)}, bf16[2,256,256]{2,1,0:T(8,128)(2,1)}, u32[]{:S(2)}) %copy-start.4) | copy-done | bytes 262168
  1.6 0.0 copy-start.6
  1.6 0.7 copy-done.6
  2.3 0.0 copy-start.8
  2.3 0.7 copy-done.8
  3.0 0.0 copy-start.11
  3.0 0.7 copy-done.11
  3.6 0.0 copy-start.13
  3.6 0.7 copy-done.13
  4.3 0.0 copy-start.15
  4.3 0.7 copy-done.15
  5.0 0.0 copy-start.17
  5.0 0.7 copy-done.17
  5.7 0.0 copy-start.2
  5.7 1.0 %spread.1 = (f32[1024,128]{1,0:T(8,128)S(1)}, bf16[4,256,256]{2,1,0:T(8,128)(2,1)S(1)}) custom-call(f32[1,1,256]{2,1,0:T(1,128)S(1)} %copy-done.11, f32[3,1,1,256]{3,2,1,0:T(1,128)S(1)} %copy-done.6, s32[1,1,256]{2,1,0:T(1,128)S(1)} %copy-done.13, s32[1,1,256]{2,1,0:T(1,128)S(1)} %copy-done.15, f32[3,1,1,256]{3,2,1,0:T(1,128)S(1)} %copy-done.8, ...), custom_call_target="tpu_custom_call" | custom-call | tf_op jit(solution)/shard_map/spread/pallas_call | solution.py:249
  6.6 0.0 copy-start
  6.7 0.0 copy-start.1
  6.7 0.0 copy-start.5
  6.7 0.0 copy-start.10
  6.7 43.5 %all_to_all.10 = f32[512,2,128]{2,1,0:T(2,128)S(1)} all-to-all(f32[512,2,128]{2,1,0:T(2,128)S(1)} %bitcast.7), channel_id=1, replica_groups=mesh['gx'=16,'gy'=32] {'gx','gy'}, dimensions={0} | all-to-all | bytes 1048576 | tf_op jit(solution)/shard_map/all_to_all | solution.py:229
  50.2 0.0 copy-done.2
  50.2 0.0 copy-done
  50.2 0.0 copy-done.1
  50.2 0.0 copy-done.5
  50.2 0.0 copy-done.10
  50.2 0.0 copy-start.3
  50.2 1.0 %copy-done.3 = bf16[2,304,256]{2,1,0:T(8,128)(2,1)S(1)} copy-done((bf16[2,304,256]{2,1,0:T(8,128)(2,1)S(1)}, bf16[2,304,256]{2,1,0:T(8,128)(2,1)}, u32[]{:S(2)}) %copy-start.3) | copy-done | bytes 311320
  51.2 3.9 %plane.1 = f32[1024,128]{1,0:T(8,128)S(1)} custom-call(f32[1024,128]{1,0:T(8,128)S(1)} %bitcast.4, bf16[2,304,256]{2,1,0:T(8,128)(2,1)S(1)} %copy-done.3, bf16[2,256,304]{2,1,0:T(8,128)(2,1)S(1)} %copy-done.1, bf16[2,352,256]{2,1,0:T(8,128)(2,1)S(1)} %copy-done.2, bf16[2,256,352]{2,1,0:T(8,128)(2,1)S(1)} %copy-done, f32[2,256]{1,0:T(2,128)S(1)} %copy-done.10, ...), custom_call_target="tpu_custom_call" | custom-call | tf_op jit(solution)/shard_map/plane/pallas_call | solution.py:262
  55.2 0.0 copy-start.9
  55.2 0.0 copy-start.12
  55.2 0.0 copy-start.14
  55.2 0.0 copy-start.16
  55.2 31.5 %all_to_all.11 = f32[512,2,128]{2,1,0:T(2,128)S(1)} all-to-all(f32[512,2,128]{2,1,0:T(2,128)S(1)} %bitcast.5), channel_id=1, replica_groups=mesh['gx'=16,'gy'=32] {'gx','gy'}, dimensions={0} | all-to-all | bytes 1048576 | tf_op jit(solution)/shard_map/all_to_all | solution.py:229
  86.7 0.0 copy-start.7
  86.7 0.0 copy-done.9
  86.7 0.0 copy-done.12
  86.7 0.0 copy-done.14
  86.7 0.0 copy-done.16
  86.7 0.7 copy-done.7
  87.4 1.2 %sample.1 = (f32[3,1,1,256]{3,2,1,0:T(1,128)}, f32[1,1,256]{2,1,0:T(1,128)}, f32[1,1,256]{2,1,0:T(1,128)}) custom-call(f32[1024,128]{1,0:T(8,128)S(1)} %bitcast.6, bf16[4,256,256]{2,1,0:T(8,128)(2,1)S(1)} %get-tuple-element.6.spectral, f32[1,1,256]{2,1,0:T(1,128)S(1)} %copy-done.12, f32[3,1,1,256]{3,2,1,0:T(1,128)S(1)} %copy-done.7, ...), custom_call_target="tpu_custom_call" | custom-call | tf_op jit(solution)/shard_map/sample/pallas_call | solution.py:281
Async XLA Ops:
  0.6 1.0 %copy-start.4 = (bf16[2,256,256]{2,1,0:T(8,128)(2,1)S(1)}, bf16[2,256,256]{2,1,0:T(8,128)(2,1)}, u32[]{:S(2)}) copy-start(bf16[2,256,256]{2,1,0:T(8,128)(2,1)} %constant.14.clone.hartley) | copy-start | bytes 786436
  1.6 0.7 copy-start.6
  2.3 0.7 copy-start.8
  3.0 0.7 copy-start.11
  3.6 0.7 copy-start.13
  4.3 0.7 copy-start.15
  5.0 0.7 copy-start.17
  5.7 44.5 %copy-start.2 = (bf16[2,352,256]{2,1,0:T(8,128)(2,1)S(1)}, bf16[2,352,256]{2,1,0:T(8,128)(2,1)}, u32[]{:S(2)}) copy-start(bf16[2,352,256]{2,1,0:T(8,128)(2,1)} %constant.17.clone.hy) | copy-start | bytes 1081348
  6.6 43.6 %copy-start = (bf16[2,256,352]{2,1,0:T(8,128)(2,1)S(1)}, bf16[2,256,352]{2,1,0:T(8,128)(2,1)}, u32[]{:S(2)}) copy-start(bf16[2,256,352]{2,1,0:T(8,128)(2,1)} %constant.18.clone.hyt) | copy-start | bytes 1081348
  6.7 43.5 %copy-start.1 = (bf16[2,256,304]{2,1,0:T(8,128)(2,1)S(1)}, bf16[2,256,304]{2,1,0:T(8,128)(2,1)}, u32[]{:S(2)}) copy-start(bf16[2,256,304]{2,1,0:T(8,128)(2,1)} %constant.16.clone.hxt) | copy-start | bytes 933892
  6.7 43.5 %copy-start.5 = (f32[256,2]{1,0:T(8,128)S(1)}, f32[256,2]{1,0:T(8,128)}, u32[]{:S(2)}) copy-start(f32[256,2]{1,0:T(8,128)} %constant.20.clone.column_terms) | copy-start | bytes 6148
  6.7 43.5 %copy-start.10 = (f32[2,256]{1,0:T(2,128)S(1)}, f32[2,256]{1,0:T(2,128)}, u32[]{:S(2)}) copy-start(f32[2,256]{1,0:T(2,128)} %constant.19.clone.row_terms.scalar_terms) | copy-start | bytes 6148
  50.2 1.0 %copy-start.3 = (bf16[2,304,256]{2,1,0:T(8,128)(2,1)S(1)}, bf16[2,304,256]{2,1,0:T(8,128)(2,1)}, u32[]{:S(2)}) copy-start(bf16[2,304,256]{2,1,0:T(8,128)(2,1)} %constant.15.clone.hx) | copy-start | bytes 933892
  55.2 31.6 %copy-start.9 = (f32[3,1,1,256]{3,2,1,0:T(1,128)S(1)}, f32[3,1,1,256]{3,2,1,0:T(1,128)}, u32[]{:S(2)}) copy-start(f32[3,1,1,256]{3,2,1,0:T(1,128)} %force_cot.3) | copy-start | bytes 9220
  55.2 31.6 %copy-start.12 = (f32[1,1,256]{2,1,0:T(1,128)S(1)}, f32[1,1,256]{2,1,0:T(1,128)}, u32[]{:S(2)}) copy-start(f32[1,1,256]{2,1,0:T(1,128)} %charge.3) | copy-start | bytes 3076
  55.2 31.6 %copy-start.14 = (s32[1,1,256]{2,1,0:T(1,128)S(1)}, s32[1,1,256]{2,1,0:T(1,128)}, u32[]{:S(2)}) copy-start(s32[1,1,256]{2,1,0:T(1,128)} %base_cell.3) | copy-start | bytes 3076
  55.2 31.5 %copy-start.16 = (s32[1,1,256]{2,1,0:T(1,128)S(1)}, s32[1,1,256]{2,1,0:T(1,128)}, u32[]{:S(2)}) copy-start(s32[1,1,256]{2,1,0:T(1,128)} %live_slot.3) | copy-start | bytes 3076
  86.7 0.7 copy-start.7
where the time goes:
time: 89 us; the launch traced here: 88.6 us
  blocking collectives  75 us (84%)
  local copies, waits for them, and re-layouts  6.71 us (8%)
  Pallas kernels  6.12 us (7%)
    all_to_all x2, blocking collectives, exchange(): lax.all_to_all(blocks.reshape(DEVICES, 2, LANES), ('gx', 'gy'), split_axi...  75 us
    unnamed x36, local copies, waits for them, and re-layouts  6.71 us
    pallas_call x1, Pallas kernels, on_device(): pl.pallas_call(plane_kernel, out_shape=message, in_specs=[vmem] * 7 + [sm...  3.95 us

commit v1 on v0

--- a/solution.py
+++ b/solution.py
@@ -19,6 +19,7 @@
 ATOMS = 256
 DEVICES = N_GX * N_GY
 LANES = 128
+PAD = 384
 
 EWALD_SPLIT = 0.8
 
@@ -34,12 +35,11 @@
     return np.stack([high, low])
 
 
-def extended_coordinates():
+def plane_coordinates():
     gx, a = np.meshgrid(np.arange(N_GX), np.arange(EX), indexing="ij")
     ext_x = (gx * CX + a - 1).reshape(-1) % K
-    b, gy = np.meshgrid(np.arange(EY), np.arange(N_GY), indexing="ij")
-    ext_y = (gy * CY + b - 1).reshape(-1) % K
-    return ext_x, ext_y
+    m, gy = np.meshgrid(np.arange(CY), np.arange(N_GY), indexing="ij")
+    return ext_x, (gy * CY + m).reshape(-1)
 
 
 def influence_factors():
@@ -106,24 +106,48 @@
 
 
 def spread_kernel(
+    charge_in, fraction_in, cell_in, live_in, force_in, potential_in, hartley_in,
+    hx_in, hyt_in, hy_in, hxt_in, rows_in, columns_in,
+    send, spectral, atoms, hx, hyt, hy, hxt, row_terms, column_terms,
     charge, fraction, base_cell, live_slot, force_cot, potential_cot, hartley,
-    send, spectral, table_a, table_b, table_c,
+    table_a, table_b, table_c, arrived,
 ):
-    live = live_slot[0].astype(jnp.float32)
-    live_charge = charge[0] * live
+    pairs = (
+        (cell_in, base_cell),
+        (fraction_in, fraction),
+        (hartley_in, hartley),
+        (charge_in, charge),
+        (live_in, live_slot),
+        (force_in, force_cot),
+        (potential_in, potential_cot),
+        (hx_in, hx),
+        (hyt_in, hyt),
+        (hy_in, hy),
+        (hxt_in, hxt),
+        (rows_in, row_terms),
+        (columns_in, column_terms),
+    )
+    copies = [
+        pltpu.make_async_copy(source, target, arrived.at[index])
+        for index, (source, target) in enumerate(pairs)
+    ]
+    for copy in copies:
+        copy.start()
+    copies[0].wait()
+    copies[1].wait()
     cells = base_cell[0]
     slot = lax.broadcasted_iota(jnp.int32, (1, ATOMS), 1)
     base_z = jnp.bitwise_and(slot, -16) + jnp.bitwise_and(cells, 15)
     wz, dz = banded(base_z - 1, spline_terms(fraction[2, 0]), K, True)
+    wx, dx, wy, dy = domain_tables(cells, fraction)
+    copies[2].wait()
     hart = (hartley[0], hartley[1])
     zw = split(product(hart, split(wz)))
     zd = split(product(hart, split(dz)))
-    spectral[0] = zw[0]
-    spectral[1] = zw[1]
-    spectral[2] = zd[0]
-    spectral[3] = zd[1]
-
-    wx, dx, wy, dy = domain_tables(cells, fraction)
+    for copy in copies[3:7]:
+        copy.wait()
+    live = live_slot[0].astype(jnp.float32)
+    live_charge = charge[0] * live
     along_x = -live_charge * force_cot[0, 0]
     along_y = -live_charge * force_cot[1, 0]
     along_z = -live_charge * force_cot[2, 0]
@@ -146,33 +170,62 @@
             send[pl.ds(field * 2 * K + half, K, stride=2), :] = value[
                 :, half * LANES : (half + 1) * LANES
             ]
+    spectral[0] = zw[0]
+    spectral[1] = zw[1]
+    spectral[2] = zd[0]
+    spectral[3] = zd[1]
+    atoms[0:24, :] = wx
+    atoms[24:48, :] = dx
+    atoms[48:64, :] = wy
+    atoms[64:80, :] = dy
+    for row, value in enumerate((live, live_charge, force_cot[0, 0], force_cot[1, 0], force_cot[2, 0])):
+        atoms[80 + row : 81 + row, :] = value
+    for copy in copies[7:]:
+        copy.wait()
 
 
 def plane_kernel(
-    received, hx, hxt, hy, hyt, row_terms, column_terms, scalar_terms, send, plane, blocks
+    received, hx, hyt, hy, hxt, row_terms, column_terms, send, plane, edges, blocks
 ):
     device = lax.axis_index("gx") * N_GY + lax.axis_index("gy")
     freq_z = lax.rem(device, K)
-    plane[:, 256:384] = jnp.zeros((EY * N_GY, LANES), jnp.float32)
+    here = lax.broadcasted_iota(jnp.int32, (1, K), 1) == freq_z
+    factor_z = jnp.sum(jnp.where(here, row_terms[0:1, :], 0.0), axis=1, keepdims=True)
+    square_z = jnp.sum(jnp.where(here, row_terms[1:2, :], 0.0), axis=1, keepdims=True)
+
+    def block(ref_main, ref_edge, b):
+        if 1 <= b <= CY:
+            return ref_main, (b - 1) * N_GY
+        return ref_edge, (0 if b == 0 else b - CY) * N_GY
+
+    plane[:, 256:PAD] = jnp.zeros((K, PAD - 256), jnp.float32)
+    edges[:, 256:PAD] = jnp.zeros((3 * N_GY, PAD - 256), jnp.float32)
     for gx in range(N_GX):
         rows = jnp.concatenate(
             [received[pl.ds(gx * 2 * N_GY + half, N_GY, stride=2), :] for half in range(2)], axis=1
         )
         for b in range(EY):
-            plane[b * N_GY : (b + 1) * N_GY, gx * EX : (gx + 1) * EX] = rows[
-                :, b * EX : (b + 1) * EX
-            ]
-    mesh_plane = plane[:, : N_GX * EX]
-    half_way = product(split(mesh_plane), (hx[0], hx[1]))
+            ref, start = block(plane, edges, b)
+            ref[start : start + N_GY, gx * EX : (gx + 1) * EX] = rows[:, b * EX : (b + 1) * EX]
+    for edge, m, shift in ((0, 7, N_GY - 1), (1, 0, 1), (2, 1, 1)):
+        plane[m * N_GY : (m + 1) * N_GY, :] += pltpu.roll(
+            edges[edge * N_GY : (edge + 1) * N_GY, :], shift, 0
+        )
+    half_way = product(split(plane[...]), (hx[0], hx[1]))
     spectrum = product((hyt[0], hyt[1]), split(half_way))
-    total_sq = (column_terms[:, 1:2] + row_terms[1:2, :]) + scalar_terms[1, freq_z]
-    factor = column_terms[:, 0:1] * (row_terms[0:1, :] * (scalar_terms[0, freq_z] / (math.pi * K)))
+    total_sq = (column_terms[:, 1:2] + row_terms[1:2, :]) + square_z
+    factor = column_terms[:, 0:1] * (row_terms[0:1, :] * (factor_z * (1.0 / (math.pi * K))))
     kernel = jnp.where(total_sq > 0.0, factor / jnp.maximum(total_sq, 1.0), 0.0)
     half_way = product((hy[0], hy[1]), split(spectrum * kernel))
-    plane[:, : N_GX * EX] = product(split(half_way), (hxt[0], hxt[1]))
+    plane[...] = product(split(half_way), (hxt[0], hxt[1]))
+    for edge, m, shift in ((0, 7, 1), (1, 0, N_GY - 1), (2, 1, N_GY - 1)):
+        edges[edge * N_GY : (edge + 1) * N_GY, :] = pltpu.roll(
+            plane[m * N_GY : (m + 1) * N_GY, :], shift, 0
+        )
     blocks[:, LANES:] = jnp.zeros((DEVICES, LANES), jnp.float32)
     for b in range(EY):
-        rows = plane[b * N_GY : (b + 1) * N_GY, :]
+        ref, start = block(plane, edges, b)
+        rows = ref[start : start + N_GY, :]
         for gx in range(N_GX):
             blocks[gx * N_GY : (gx + 1) * N_GY, b * EX : (b + 1) * EX] = rows[
                 :, gx * EX : (gx + 1) * EX
@@ -182,8 +235,7 @@
 
 
 def sample_kernel(
-    received, spectral, charge, fraction, base_cell, live_slot, force_cot,
-    forces, potential, charge_grad, sample_a, sample_b, sample_c,
+    received, spectral, atoms, forces, potential, charge_grad, sample_a, sample_b, sample_c
 ):
     def field(index):
         halves = [received[pl.ds(index * 2 * K + half, K, stride=2), :] for half in range(2)]
@@ -195,9 +247,8 @@
     sample_a[...] = product(first, zw)
     sample_b[...] = product(first, zd)
     sample_c[...] = product(field(1), zw)
-    live = live_slot[0].astype(jnp.float32)
-    live_charge = charge[0] * live
-    wx, dx, wy, dy = domain_tables(base_cell[0], fraction)
+    wx, dx, wy, dy = atoms[0:24, :], atoms[24:48, :], atoms[48:64, :], atoms[64:80, :]
+    live, live_charge, along_x, along_y, along_z = [atoms[80 + row : 81 + row, :] for row in range(5)]
     sums = [jnp.zeros((24, ATOMS), jnp.float32) for _ in range(5)]
     for b in range(EY):
         wyb = wy[b : b + 1]
@@ -217,12 +268,7 @@
     forces[1, 0] = -live_charge * grad_y
     forces[2, 0] = -live_charge * grad_z
     potential[0] = live * mesh_value
-    charge_grad[0] = live * (
-        response
-        - force_cot[0, 0] * grad_x
-        - force_cot[1, 0] * grad_y
-        - force_cot[2, 0] * grad_z
-    )
+    charge_grad[0] = live * (response - along_x * grad_x - along_y * grad_y - along_z * grad_z)
 
 
 def exchange(blocks):
@@ -233,50 +279,51 @@
 
 
 def on_device(charge, fraction, base_cell, live_slot, force_cot, potential_cot):
-    ext_x, ext_y = extended_coordinates()
+    x, y = plane_coordinates()
     freq = np.arange(K)
-    factor, squares = influence_factors()
-    terms = np.stack([factor, squares])
-    hx = cas_table(ext_x, freq)
-    hy = cas_table(ext_y, freq)
+    terms = np.stack(influence_factors())
+    hx = np.pad(cas_table(x, freq), ((0, PAD - x.size), (0, 0)))
+    hy = cas_table(y, freq)
+    constants = [split_table(value) for value in (hx, hy.T, hy, hx.T)] + [terms, terms.T]
     params = pltpu.CompilerParams(vmem_limit_bytes=48 * 1024 * 1024)
     vmem = pl.BlockSpec(memory_space=pltpu.VMEM)
-    smem = pl.BlockSpec(memory_space=pltpu.SMEM)
+    hbm = pl.BlockSpec(memory_space=pltpu.HBM)
     f32 = jnp.float32
     table = pltpu.VMEM((K, ATOMS), f32)
     message = jax.ShapeDtypeStruct((2 * DEVICES, LANES), f32)
-
-    sent, spectral = pl.pallas_call(
+    arguments = (charge, fraction, base_cell, live_slot, force_cot, potential_cot)
+    hartley = split_table(cas_table(freq, freq))
+
+    sent, spectral, atoms, *tables = pl.pallas_call(
         spread_kernel,
-        out_shape=(message, jax.ShapeDtypeStruct((4, K, ATOMS), jnp.bfloat16)),
-        in_specs=[vmem] * 7,
-        out_specs=(vmem, vmem),
-        scratch_shapes=[table, table, table],
+        out_shape=(
+            message,
+            jax.ShapeDtypeStruct((4, K, ATOMS), jnp.bfloat16),
+            jax.ShapeDtypeStruct((88, ATOMS), f32),
+            *[jax.ShapeDtypeStruct(value.shape, value.dtype) for value in constants],
+        ),
+        in_specs=[hbm] * 13,
+        out_specs=(vmem,) * 9,
+        scratch_shapes=[pltpu.VMEM(value.shape, value.dtype) for value in arguments]
+        + [pltpu.VMEM(hartley.shape, hartley.dtype), table, table, table]
+        + [pltpu.SemaphoreType.DMA((13,))],
         compiler_params=params,
         name="spread",
-    )(
-        charge, fraction, base_cell, live_slot, force_cot, potential_cot,
-        jnp.asarray(split_table(cas_table(freq, freq))),
-    )
+    )(*arguments, jnp.asarray(hartley), *[jnp.asarray(value) for value in constants])
     received = exchange(sent)
     solved = pl.pallas_call(
         plane_kernel,
         out_shape=message,
-        in_specs=[vmem] * 7 + [smem],
+        in_specs=[vmem] * 7,
         out_specs=vmem,
-        scratch_shapes=[pltpu.VMEM((EY * N_GY, 384), f32), pltpu.VMEM((DEVICES, 2 * LANES), f32)],
+        scratch_shapes=[
+            pltpu.VMEM((K, PAD), f32),
+            pltpu.VMEM((3 * N_GY, PAD), f32),
+            pltpu.VMEM((DEVICES, 2 * LANES), f32),
+        ],
         compiler_params=params,
         name="plane",
-    )(
-        received,
-        jnp.asarray(split_table(hx)),
-        jnp.asarray(split_table(hx.T)),
-        jnp.asarray(split_table(hy)),
-        jnp.asarray(split_table(hy.T)),
-        jnp.asarray(terms),
-        jnp.asarray(terms.T),
-        jnp.asarray(terms),
-    )
+    )(received, *tables)
     returned = exchange(solved)
     return pl.pallas_call(
         sample_kernel,
@@ -285,12 +332,12 @@
             jax.ShapeDtypeStruct((1, 1, ATOMS), f32),
             jax.ShapeDtypeStruct((1, 1, ATOMS), f32),
         ),
-        in_specs=[vmem] * 7,
+        in_specs=[vmem] * 3,
         out_specs=(vmem, vmem, vmem),
         scratch_shapes=[table, table, table],
         compiler_params=params,
         name="sample",
-    )(returned, spectral, charge, fraction, base_cell, live_slot, force_cot)
+    )(returned, spectral, atoms)
 
 
 def solution(mesh):

time: 89 us -> 93.2 us (1.047)
  local copies, waits for them, and re-layouts: 6.71 us -> 10.5 us
    unnamed x36 -> x26, local copies, waits for them, and re-layouts: 6.71 us -> 10.5 us
    pallas_call x1, Pallas kernels: 0.97 us -> 2.11 us  [on_device(): pl.pallas_call(spread_kernel, out_shape=(message, jax.ShapeDtypeStruct((4...]
where the time goes in v1:
time: 93.2 us; the launch traced here: 92.7 us
  blocking collectives  75 us (80%)
  local copies, waits for them, and re-layouts  10.5 us (11%)
  Pallas kernels  6.55 us (7%)
    all_to_all x2, blocking collectives, exchange(): lax.all_to_all(blocks.reshape(DEVICES, 2, LANES), ('gx', 'gy'), split_axi...  75 us
    unnamed x26, local copies, waits for them, and re-layouts  10.5 us
    pallas_call x1, Pallas kernels, on_device(): pl.pallas_call(plane_kernel, out_shape=message, in_specs=[vmem] * 7, out_...  3.26 us
    pallas_call x1, Pallas kernels, on_device(): pl.pallas_call(spread_kernel, out_shape=(message, jax.ShapeDtypeStruct((4...  2.11 us

profile of v1, /device:TPU:1, one launch (start us, length us, event | category | flops | bytes accessed | tf_op | source)
XLA Modules:
  0.0 92.7 jit_solution(13036138129015148376)
XLA Ops:
  0.6 0.0 copy-start.8
  0.6 0.7 copy-done.8
  1.3 0.0 copy-start
  1.3 1.0 %copy-done = bf16[2,256,384]{2,1,0:T(8,128)(2,1)S(1)} copy-done((bf16[2,256,384]{2,1,0:T(8,128)(2,1)S(1)}, bf16[2,256,384]{2,1,0:T(8,128)(2,1)}, u32[]{:S(2)}) %copy-start) | copy-done | bytes 393240
  2.3 0.0 copy-start.1
  2.3 1.0 %copy-done.1 = bf16[2,384,256]{2,1,0:T(8,128)(2,1)S(1)} copy-done((bf16[2,384,256]{2,1,0:T(8,128)(2,1)S(1)}, bf16[2,384,256]{2,1,0:T(8,128)(2,1)}, u32[]{:S(2)}) %copy-start.1) | copy-done | bytes 393240
  3.3 0.0 copy-start.2
  3.3 0.9 %copy-done.2 = bf16[2,256,256]{2,1,0:T(8,128)(2,1)S(1)} copy-done((bf16[2,256,256]{2,1,0:T(8,128)(2,1)S(1)}, bf16[2,256,256]{2,1,0:T(8,128)(2,1)}, u32[]{:S(2)}) %copy-start.2) | copy-done | bytes 262168
  4.3 0.0 copy-start.3
  4.3 0.9 %copy-done.3 = bf16[2,256,256]{2,1,0:T(8,128)(2,1)S(1)} copy-done((bf16[2,256,256]{2,1,0:T(8,128)(2,1)S(1)}, bf16[2,256,256]{2,1,0:T(8,128)(2,1)}, u32[]{:S(2)}) %copy-start.3) | copy-done | bytes 262168
  5.2 0.0 copy-start.4
  5.2 0.9 %copy-done.4 = bf16[2,256,256]{2,1,0:T(8,128)(2,1)S(1)} copy-done((bf16[2,256,256]{2,1,0:T(8,128)(2,1)S(1)}, bf16[2,256,256]{2,1,0:T(8,128)(2,1)}, u32[]{:S(2)}) %copy-start.4) | copy-done | bytes 262168
  6.2 0.0 copy-start.5
  6.2 0.9 copy-done.5
  7.1 0.0 copy-start.6
  7.1 0.7 copy-done.6
  7.8 0.0 copy-start.7
  7.8 0.7 copy-done.7
  8.4 0.0 copy-start.9
  8.4 0.7 copy-done.9
  9.1 0.0 copy-start.10
  9.1 0.7 copy-done.10
  9.8 0.0 copy-start.11
  9.8 0.7 copy-done.11
  10.5 0.0 copy-start.12
  10.5 0.7 copy-done.12
  11.2 2.1 %spread.1 = (f32[1024,128]{1,0:T(8,128)S(1)}, bf16[4,256,256]{2,1,0:T(8,128)(2,1)S(1)}, f32[88,256]{1,0:T(8,128)S(1)}, bf16[2,384,256]{2,1,0:T(8,128)(2,1)S(1)},...) custom-call(f32[1,1,256]{2,1,0:T(1,128)S(1)} %copy-done.9, ...), custom_call_target="tpu_custom_call" | custom-call | tf_op jit(solution)/shard_map/spread/pallas_call | solution.py:297
  13.3 43.5 %all_to_all.10 = f32[512,2,128]{2,1,0:T(2,128)S(1)} all-to-all(f32[512,2,128]{2,1,0:T(2,128)S(1)} %bitcast.7), channel_id=1, replica_groups=mesh['gx'=16,'gy'=32] {'gx','gy'}, dimensions={0} | all-to-all | bytes 1048576 | tf_op jit(solution)/shard_map/all_to_all | solution.py:275
  56.8 3.3 %plane.1 = f32[1024,128]{1,0:T(8,128)S(1)} custom-call(f32[1024,128]{1,0:T(8,128)S(1)} %bitcast.5, bf16[2,384,256]{2,1,0:T(8,128)(2,1)S(1)} %get-tuple-element.13.hx, bf16[2,256,256]{2,1,0:T(8,128)(2,1)S(1)} %get-tuple-element.14.hyt, bf16[2,256,256]{2,1,0:T(8,128)(2,1)S(1)} %get-tuple-element.15.hy, bf16[2,256,384]{2,1,0:T(8,128)(2,1)S(1)} %get-tuple-element.16.hxt, ...), custom_call_target="tpu_custom_call" | custom-call | tf_op jit(solution)/shard_map/plane/pallas_call | solution.py:314
  60.0 31.5 %all_to_all.11 = f32[512,2,128]{2,1,0:T(2,128)S(1)} all-to-all(f32[512,2,128]{2,1,0:T(2,128)S(1)} %bitcast.6), channel_id=1, replica_groups=mesh['gx'=16,'gy'=32] {'gx','gy'}, dimensions={0} | all-to-all | bytes 1048576 | tf_op jit(solution)/shard_map/all_to_all | solution.py:275
  91.5 1.2 %sample.1 = (f32[3,1,1,256]{3,2,1,0:T(1,128)}, f32[1,1,256]{2,1,0:T(1,128)}, f32[1,1,256]{2,1,0:T(1,128)}) custom-call(f32[1024,128]{1,0:T(8,128)S(1)} %bitcast.4, bf16[4,256,256]{2,1,0:T(8,128)(2,1)S(1)} %get-tuple-element.19.spectral, f32[88,256]{1,0:T(8,128)S(1)} %get-tuple-element.20.atoms), custom_call_target="tpu_custom_call" | custom-call | tf_op jit(solution)/shard_map/sample/pallas_call | solution.py:328
Async XLA Ops:
  0.6 0.7 copy-start.8
  1.3 1.0 %copy-start = (bf16[2,256,384]{2,1,0:T(8,128)(2,1)S(1)}, bf16[2,256,384]{2,1,0:T(8,128)(2,1)}, u32[]{:S(2)}) copy-start(bf16[2,256,384]{2,1,0:T(8,128)(2,1)} %constant.18.clone.hxt_in) | copy-start | bytes 1179652
  2.3 1.0 %copy-start.1 = (bf16[2,384,256]{2,1,0:T(8,128)(2,1)S(1)}, bf16[2,384,256]{2,1,0:T(8,128)(2,1)}, u32[]{:S(2)}) copy-start(bf16[2,384,256]{2,1,0:T(8,128)(2,1)} %constant.15.clone.hx_in) | copy-start | bytes 1179652
  3.3 0.9 %copy-start.2 = (bf16[2,256,256]{2,1,0:T(8,128)(2,1)S(1)}, bf16[2,256,256]{2,1,0:T(8,128)(2,1)}, u32[]{:S(2)}) copy-start(bf16[2,256,256]{2,1,0:T(8,128)(2,1)} %constant.17.clone.hy_in) | copy-start | bytes 786436
  4.3 0.9 %copy-start.3 = (bf16[2,256,256]{2,1,0:T(8,128)(2,1)S(1)}, bf16[2,256,256]{2,1,0:T(8,128)(2,1)}, u32[]{:S(2)}) copy-start(bf16[2,256,256]{2,1,0:T(8,128)(2,1)} %constant.16.clone.hyt_in) | copy-start | bytes 786436
  5.2 0.9 %copy-start.4 = (bf16[2,256,256]{2,1,0:T(8,128)(2,1)S(1)}, bf16[2,256,256]{2,1,0:T(8,128)(2,1)}, u32[]{:S(2)}) copy-start(bf16[2,256,256]{2,1,0:T(8,128)(2,1)} %constant.14.clone.hartley_in) | copy-start | bytes 786436
  6.2 0.9 copy-start.5
  7.1 0.7 copy-start.6
  7.8 0.7 copy-start.7
  8.4 0.7 copy-start.9
  9.1 0.7 copy-start.10
  9.8 0.7 copy-start.11
  10.5 0.7 copy-start.12

commit v2 on v1

--- a/solution.py
+++ b/solution.py
@@ -20,6 +20,7 @@
 DEVICES = N_GX * N_GY
 LANES = 128
 PAD = 384
+SPREAD_GRANT = 60 * 1024 * 1024
 
 EWALD_SPLIT = 0.8
 
@@ -40,6 +41,12 @@
     ext_x = (gx * CX + a - 1).reshape(-1) % K
     m, gy = np.meshgrid(np.arange(CY), np.arange(N_GY), indexing="ij")
     return ext_x, (gy * CY + m).reshape(-1)
+
+
+def natural(index):
+    return jnp.bitwise_or(
+        jnp.left_shift(jnp.bitwise_and(index, N_GY - 1), 3), jnp.right_shift(index, 5)
+    )
 
 
 def influence_factors():
@@ -83,34 +90,35 @@
     return weights, slopes
 
 
-def banded(first, terms, rows, wrap):
-    place = lax.broadcasted_iota(jnp.int32, (rows, ATOMS), 0) - first
-    if wrap:
-        place = jnp.bitwise_and(place, rows - 1)
+def banded(place, terms):
     hits = [place == offset for offset in range(4)]
 
     def table(values):
-        out = jnp.zeros((rows, ATOMS), jnp.float32)
+        out = jnp.zeros(place.shape, jnp.float32)
         for hit, value in zip(hits, values):
-            out = jnp.where(hit, jnp.broadcast_to(value, (rows, ATOMS)), out)
+            out = jnp.where(hit, jnp.broadcast_to(value, place.shape), out)
         return out
 
     return [table(values) for values in terms]
 
 
+def row_numbers(rows):
+    return lax.broadcasted_iota(jnp.int32, (rows, ATOMS), 0)
+
+
 def domain_tables(cells, fraction_ref):
-    wx, dx = banded(jnp.right_shift(cells, 7), spline_terms(fraction_ref[0, 0]), 24, False)
+    cell_x = jnp.right_shift(cells, 7)
     cell_y = jnp.bitwise_and(jnp.right_shift(cells, 4), CY - 1)
-    wy, dy = banded(cell_y, spline_terms(fraction_ref[1, 0]), 16, False)
+    wx, dx = banded(row_numbers(24) - cell_x, spline_terms(fraction_ref[0, 0]))
+    wy, dy = banded(row_numbers(16) - cell_y, spline_terms(fraction_ref[1, 0]))
     return wx, dx, wy, dy
 
 
 def spread_kernel(
     charge_in, fraction_in, cell_in, live_in, force_in, potential_in, hartley_in,
-    hx_in, hyt_in, hy_in, hxt_in, rows_in, columns_in,
-    send, spectral, atoms, hx, hyt, hy, hxt, row_terms, column_terms,
+    send_out, spectral_out, atoms_out,
     charge, fraction, base_cell, live_slot, force_cot, potential_cot, hartley,
-    table_a, table_b, table_c, arrived,
+    table_a, table_b, table_c, send, spectral, atoms, arrived, left,
 ):
     pairs = (
         (cell_in, base_cell),
@@ -120,12 +128,6 @@
         (live_in, live_slot),
         (force_in, force_cot),
         (potential_in, potential_cot),
-        (hx_in, hx),
-        (hyt_in, hyt),
-        (hy_in, hy),
-        (hxt_in, hxt),
-        (rows_in, row_terms),
-        (columns_in, column_terms),
     )
     copies = [
         pltpu.make_async_copy(source, target, arrived.at[index])
@@ -133,18 +135,36 @@
     ]
     for copy in copies:
         copy.start()
-    copies[0].wait()
-    copies[1].wait()
+    half = slice(0, 2 * K), slice(2 * K, 4 * K)
+    results = [
+        pltpu.make_async_copy(source, target, left.at[index])
+        for index, (source, target) in enumerate((
+            (send.at[half[0]], send_out.at[half[0]]),
+            (send.at[half[1]], send_out.at[half[1]]),
+            (spectral, spectral_out),
+            (atoms, atoms_out),
+        ))
+    ]
+
+    def store(field, value):
+        for part in range(2):
+            send[pl.ds(field * 2 * K + part, K, stride=2), :] = value[
+                :, part * LANES : (part + 1) * LANES
+            ]
+        results[field].start()
+
+    for copy in copies[0:2]:
+        copy.wait()
     cells = base_cell[0]
     slot = lax.broadcasted_iota(jnp.int32, (1, ATOMS), 1)
     base_z = jnp.bitwise_and(slot, -16) + jnp.bitwise_and(cells, 15)
-    wz, dz = banded(base_z - 1, spline_terms(fraction[2, 0]), K, True)
+    place_z = jnp.bitwise_and(natural(row_numbers(K)) - (base_z - 1), K - 1)
+    wz, dz = banded(place_z, spline_terms(fraction[2, 0]))
     wx, dx, wy, dy = domain_tables(cells, fraction)
     copies[2].wait()
     hart = (hartley[0], hartley[1])
     zw = split(product(hart, split(wz)))
-    zd = split(product(hart, split(dz)))
-    for copy in copies[3:7]:
+    for copy in copies[3:]:
         copy.wait()
     live = live_slot[0].astype(jnp.float32)
     live_charge = charge[0] * live
@@ -163,35 +183,37 @@
         table_b[rows, :] = dx * (along_x * wyb) + wx * (along_y * dyb + direct * wyb)
         table_c[rows, :] = wx * (along_z * wyb)
     nt = ((1,), (1,))
-    first = product(zw, split(table_a[...]), nt)
-    second = product(zw, split(table_b[...]), nt) + product(zd, split(table_c[...]), nt)
-    for field, value in enumerate((first, second)):
-        for half in range(2):
-            send[pl.ds(field * 2 * K + half, K, stride=2), :] = value[
-                :, half * LANES : (half + 1) * LANES
-            ]
+    store(0, product(zw, split(table_a[...]), nt))
+    zd = split(product(hart, split(dz)))
+    store(1, product(zw, split(table_b[...]), nt) + product(zd, split(table_c[...]), nt))
     spectral[0] = zw[0]
     spectral[1] = zw[1]
     spectral[2] = zd[0]
     spectral[3] = zd[1]
+    results[2].start()
     atoms[0:24, :] = wx
     atoms[24:48, :] = dx
     atoms[48:64, :] = wy
     atoms[64:80, :] = dy
-    for row, value in enumerate((live, live_charge, force_cot[0, 0], force_cot[1, 0], force_cot[2, 0])):
+    scalars = (live, live_charge, force_cot[0, 0], force_cot[1, 0], force_cot[2, 0])
+    for row, value in enumerate(scalars):
         atoms[80 + row : 81 + row, :] = value
-    for copy in copies[7:]:
+    atoms[85:88, :] = jnp.zeros((3, ATOMS), jnp.float32)
+    results[3].start()
+    for copy in results:
         copy.wait()
 
 
 def plane_kernel(
-    received, hx, hyt, hy, hxt, row_terms, column_terms, send, plane, edges, blocks
+    received, hartley, tables, send, plane, edges, blocks
 ):
     device = lax.axis_index("gx") * N_GY + lax.axis_index("gy")
-    freq_z = lax.rem(device, K)
-    here = lax.broadcasted_iota(jnp.int32, (1, K), 1) == freq_z
-    factor_z = jnp.sum(jnp.where(here, row_terms[0:1, :], 0.0), axis=1, keepdims=True)
-    square_z = jnp.sum(jnp.where(here, row_terms[1:2, :], 0.0), axis=1, keepdims=True)
+    here = lax.broadcasted_iota(jnp.int32, (1, K), 1) == lax.rem(device, K)
+    factor_x, square_x, factor_y, square_y = [tables[PAD + row : PAD + row + 1, :] for row in range(4)]
+    factor_z = jnp.sum(jnp.where(here, factor_y, 0.0), axis=1, keepdims=True)
+    square_z = jnp.sum(jnp.where(here, square_y, 0.0), axis=1, keepdims=True)
+    hy = (hartley[0], hartley[1])
+    hx = split(tables[0:PAD, :])
 
     def block(ref_main, ref_edge, b):
         if 1 <= b <= CY:
@@ -211,13 +233,13 @@
         plane[m * N_GY : (m + 1) * N_GY, :] += pltpu.roll(
             edges[edge * N_GY : (edge + 1) * N_GY, :], shift, 0
         )
-    half_way = product(split(plane[...]), (hx[0], hx[1]))
-    spectrum = product((hyt[0], hyt[1]), split(half_way))
-    total_sq = (column_terms[:, 1:2] + row_terms[1:2, :]) + square_z
-    factor = column_terms[:, 0:1] * (row_terms[0:1, :] * (factor_z * (1.0 / (math.pi * K))))
+    half_way = product(split(plane[...]), hx)
+    spectrum = product(hy, split(half_way))
+    total_sq = jnp.transpose(square_y) + (square_x + square_z)
+    factor = jnp.transpose(factor_y) * (factor_x * (factor_z * (1.0 / (math.pi * K))))
     kernel = jnp.where(total_sq > 0.0, factor / jnp.maximum(total_sq, 1.0), 0.0)
-    half_way = product((hy[0], hy[1]), split(spectrum * kernel))
-    plane[...] = product(split(half_way), (hxt[0], hxt[1]))
+    half_way = product(hy, split(spectrum * kernel))
+    plane[...] = product(split(half_way), hx, ((1,), (1,)))
     for edge, m, shift in ((0, 7, 1), (1, 0, N_GY - 1), (2, 1, N_GY - 1)):
         edges[edge * N_GY : (edge + 1) * N_GY, :] = pltpu.roll(
             plane[m * N_GY : (m + 1) * N_GY, :], shift, 0
@@ -281,10 +303,11 @@
 def on_device(charge, fraction, base_cell, live_slot, force_cot, potential_cot):
     x, y = plane_coordinates()
     freq = np.arange(K)
-    terms = np.stack(influence_factors())
-    hx = np.pad(cas_table(x, freq), ((0, PAD - x.size), (0, 0)))
-    hy = cas_table(y, freq)
-    constants = [split_table(value) for value in (hx, hy.T, hy, hx.T)] + [terms, terms.T]
+    hartley = split_table(cas_table(y, y))
+    factor, square = influence_factors()
+    tables = np.zeros((PAD + 8, K), np.float32)
+    tables[: x.size] = cas_table(x, freq)
+    tables[PAD : PAD + 4] = factor, square, factor[y], square[y]
     params = pltpu.CompilerParams(vmem_limit_bytes=48 * 1024 * 1024)
     vmem = pl.BlockSpec(memory_space=pltpu.VMEM)
     hbm = pl.BlockSpec(memory_space=pltpu.HBM)
@@ -292,29 +315,28 @@
     table = pltpu.VMEM((K, ATOMS), f32)
     message = jax.ShapeDtypeStruct((2 * DEVICES, LANES), f32)
     arguments = (charge, fraction, base_cell, live_slot, force_cot, potential_cot)
-    hartley = split_table(cas_table(freq, freq))
-
-    sent, spectral, atoms, *tables = pl.pallas_call(
+
+    sent, spectral, atoms = pl.pallas_call(
         spread_kernel,
         out_shape=(
             message,
             jax.ShapeDtypeStruct((4, K, ATOMS), jnp.bfloat16),
             jax.ShapeDtypeStruct((88, ATOMS), f32),
-            *[jax.ShapeDtypeStruct(value.shape, value.dtype) for value in constants],
         ),
-        in_specs=[hbm] * 13,
-        out_specs=(vmem,) * 9,
+        in_specs=[hbm] * 7,
+        out_specs=(hbm,) * 3,
         scratch_shapes=[pltpu.VMEM(value.shape, value.dtype) for value in arguments]
         + [pltpu.VMEM(hartley.shape, hartley.dtype), table, table, table]
-        + [pltpu.SemaphoreType.DMA((13,))],
-        compiler_params=params,
+        + [pltpu.VMEM((2 * DEVICES, LANES), f32), pltpu.VMEM((4, K, ATOMS), jnp.bfloat16)]
+        + [pltpu.VMEM((88, ATOMS), f32), pltpu.SemaphoreType.DMA((7,)), pltpu.SemaphoreType.DMA((4,))],
+        compiler_params=pltpu.CompilerParams(vmem_limit_bytes=SPREAD_GRANT),
         name="spread",
-    )(*arguments, jnp.asarray(hartley), *[jnp.asarray(value) for value in constants])
+    )(*arguments, jnp.asarray(hartley))
     received = exchange(sent)
     solved = pl.pallas_call(
         plane_kernel,
         out_shape=message,
-        in_specs=[vmem] * 7,
+        in_specs=[vmem] * 3,
         out_specs=vmem,
         scratch_shapes=[
             pltpu.VMEM((K, PAD), f32),
@@ -323,7 +345,7 @@
         ],
         compiler_params=params,
         name="plane",
-    )(received, *tables)
+    )(received, jnp.asarray(hartley), jnp.asarray(tables))
     returned = exchange(solved)
     return pl.pallas_call(
         sample_kernel,

time: 93.2 us -> 83.8 us (0.90)
  local copies, waits for them, and re-layouts: 10.5 us -> 0.02 us
  Pallas kernels: 6.55 us -> 7.56 us
    unnamed x26 -> x8, local copies, waits for them, and re-layouts: 10.5 us -> 0.02 us
    pallas_call x1, Pallas kernels: 2.11 us -> 3.1 us  [on_device(): pl.pallas_call(spread_kernel, out_shape=(message, jax.ShapeDtypeStruct((4...]
where the time goes in v2:
time: 83.8 us; the launch traced here: 83.6 us
  blocking collectives  75.4 us (90%)
  Pallas kernels  7.56 us (9%)
    all_to_all x2, blocking collectives, exchange(): lax.all_to_all(blocks.reshape(DEVICES, 2, LANES), ('gx', 'gy'), split_axi...  75.4 us
    pallas_call x1, Pallas kernels, on_device(): pl.pallas_call(plane_kernel, out_shape=message, in_specs=[vmem] * 3, out_...  3.26 us
    pallas_call x1, Pallas kernels, on_device(): pl.pallas_call(spread_kernel, out_shape=(message, jax.ShapeDtypeStruct((4...  3.1 us

profile of v2, /device:TPU:1, one launch (start us, length us, event | category | flops | bytes accessed | tf_op | source)
XLA Modules:
  0.0 83.6 jit_solution(8830186556177106544)
XLA Ops:
  0.6 3.1 %spread.1 = (f32[1024,128]{1,0:T(8,128)}, bf16[4,256,256]{2,1,0:T(8,128)(2,1)}, f32[88,256]{1,0:T(8,128)}) custom-call(f32[1,1,256]{2,1,0:T(1,128)} %charge_in.1, f32[3,1,1,256]{3,2,1,0:T(1,128)} %fraction_in.1, s32[1,1,256]{2,1,0:T(1,128)} %cell_in.1, s32[1,1,256]{2,1,0:T(1,128)} %live_in.1, f32[3,1,1,256]{3,2,1,0:T(1,128)} %force_in.1, ...), custom_call_target="tpu_custom_call" | custom-call | tf_op jit(solution)/shard_map/spread/pallas_call | solution.py:319
  3.7 0.0 copy-start
  3.8 0.0 copy-start.2
  3.8 43.7 %all_to_all.10 = f32[512,2,128]{2,1,0:T(2,128)S(1)} all-to-all(f32[512,2,128]{2,1,0:T(2,128)} %bitcast.7), channel_id=1, replica_groups=mesh['gx'=16,'gy'=32] {'gx','gy'}, dimensions={0} | all-to-all | bytes 1048576 | tf_op jit(solution)/shard_map/all_to_all | solution.py:297
  47.5 0.0 copy-done
  47.5 0.0 copy-done.2
  47.5 3.3 %plane.1 = f32[1024,128]{1,0:T(8,128)S(1)} custom-call(f32[1024,128]{1,0:T(8,128)S(1)} %bitcast.5, bf16[2,256,256]{2,1,0:T(8,128)(2,1)S(1)} %copy-done, f32[392,256]{1,0:T(8,128)S(1)} %copy-done.2), custom_call_target="tpu_custom_call" | custom-call | tf_op jit(solution)/shard_map/plane/pallas_call | solution.py:336
  50.8 0.0 copy-start.1
  50.8 0.0 copy-start.3
  50.8 31.6 %all_to_all.11 = f32[512,2,128]{2,1,0:T(2,128)S(1)} all-to-all(f32[512,2,128]{2,1,0:T(2,128)S(1)} %bitcast.6), channel_id=1, replica_groups=mesh['gx'=16,'gy'=32] {'gx','gy'}, dimensions={0} | all-to-all | bytes 1048576 | tf_op jit(solution)/shard_map/all_to_all | solution.py:297
  82.4 0.0 copy-done.1
  82.4 0.0 copy-done.3
  82.4 1.2 %sample.1 = (f32[3,1,1,256]{3,2,1,0:T(1,128)}, f32[1,1,256]{2,1,0:T(1,128)}, f32[1,1,256]{2,1,0:T(1,128)}) custom-call(f32[1024,128]{1,0:T(8,128)S(1)} %bitcast.4, bf16[4,256,256]{2,1,0:T(8,128)(2,1)S(1)} %copy-done.1, f32[88,256]{1,0:T(8,128)S(1)} %copy-done.3), custom_call_target="tpu_custom_call" | custom-call | tf_op jit(solution)/shard_map/sample/pallas_call | solution.py:350
Async XLA Ops:
  3.7 43.8 %copy-start = (bf16[2,256,256]{2,1,0:T(8,128)(2,1)S(1)}, bf16[2,256,256]{2,1,0:T(8,128)(2,1)}, u32[]{:S(2)}) copy-start(bf16[2,256,256]{2,1,0:T(8,128)(2,1)} %constant.4.clone.hartley_in.hartley) | copy-start | bytes 786436
  3.8 43.8 %copy-start.2 = (f32[392,256]{1,0:T(8,128)S(1)}, f32[392,256]{1,0:T(8,128)}, u32[]{:S(2)}) copy-start(f32[392,256]{1,0:T(8,128)} %constant.5.clone.tables) | copy-start | bytes 1204228
  50.8 31.7 %copy-start.1 = (bf16[4,256,256]{2,1,0:T(8,128)(2,1)S(1)}, bf16[4,256,256]{2,1,0:T(8,128)(2,1)}, u32[]{:S(2)}) copy-start(bf16[4,256,256]{2,1,0:T(8,128)(2,1)} %get-tuple-element.7.spectral) | copy-start | bytes 1572868
  50.8 31.6 %copy-start.3 = (f32[88,256]{1,0:T(8,128)S(1)}, f32[88,256]{1,0:T(8,128)}, u32[]{:S(2)}) copy-start(f32[88,256]{1,0:T(8,128)} %get-tuple-element.8.atoms) | copy-start | bytes 270340

commit v3 on v2

v3 whole, which is shorter than its diff:
```python
import math

import jax
import jax.numpy as jnp
import ml_dtypes
import numpy as np
from jax import lax
from jax.experimental import pallas as pl
from jax.experimental.pallas import tpu as pltpu
from jax.sharding import PartitionSpec as P

K = 256
CY = 8
N_GX = 16
N_GY = 32
ATOMS = 256
DEVICES = N_GX * N_GY
LANES = 128
SCALARS = 256
SPREAD_GRANT = 60 * 1024 * 1024

EWALD_SPLIT = 0.8


def cas_table(left, right):
    angles = 2.0 * math.pi / K * (left[:, None] * right[None, :] % K)
    return np.cos(angles) + np.sin(angles)


def split_table(table):
    high = table.astype(np.float32).astype(ml_dtypes.bfloat16)
    low = (table - high.astype(np.float64)).astype(np.float32).astype(ml_dtypes.bfloat16)
    return np.stack([high, low])


def plane_rows():
    m, gy = np.meshgrid(np.arange(CY), np.arange(N_GY), indexing="ij")
    return (gy * CY + m).reshape(-1)


def natural(index):
    return jnp.bitwise_or(
        jnp.left_shift(jnp.bitwise_and(index, N_GY - 1), 3), jnp.right_shift(index, 5)
    )


def influence_factors():
    freq = np.arange(K)
    nearest = np.minimum(freq, K - freq).astype(np.float64)
    damping = math.pi * math.pi / (EWALD_SPLIT * EWALD_SPLIT * K * K)
    cosine = np.cos(2.0 * math.pi / K * freq)
    factor = np.exp(-damping * nearest * nearest) * 9.0 / (2.0 + cosine) ** 2
    return factor.astype(np.float32), (nearest * nearest).astype(np.float32)


def split(value):
    high = value.astype(jnp.bfloat16)
    low = (value - high.astype(jnp.float32)).astype(jnp.bfloat16)
    return high, low


def product(left, right, dims=((1,), (0,))):
    def one(a, b):
        return lax.dot_general(a, b, (dims, ((), ())), preferred_element_type=jnp.float32)

    return one(left[0], right[0]) + (one(left[0], right[1]) + one(left[1], right[0]))


def spline_terms(fraction):
    square = fraction * fraction
    cubic_part = square * fraction
    remain = 1.0 - fraction
    weights = (
        remain * remain * remain * (1.0 / 6.0),
        (3.0 * cubic_part - 6.0 * square + 4.0) * (1.0 / 6.0),
        (-3.0 * cubic_part + 3.0 * square + 3.0 * fraction + 1.0) * (1.0 / 6.0),
        cubic_part * (1.0 / 6.0),
    )
    slopes = (
        -0.5 * remain * remain,
        (3.0 * square - 4.0 * fraction) * 0.5,
        (-3.0 * square + 2.0 * fraction + 1.0) * 0.5,
        0.5 * square,
    )
    return weights, slopes


def banded(place, terms):
    hits = [place == offset for offset in range(4)]

    def table(values):
        out = jnp.zeros(place.shape, jnp.float32)
        for hit, value in zip(hits, values):
            out = jnp.where(hit, jnp.broadcast_to(value, place.shape), out)
        return out

    return [table(values) for values in terms]


def row_numbers(rows):
    return lax.broadcasted_iota(jnp.int32, (rows, ATOMS), 0)


SHIFT_X = 53
SHIFT_XY = 57
EDGES = {0: 8, 1: 9, 7: -1}


def halo_x(lane):
    low = (lane == 15) | (lane == 4) | (lane == 8)
    upper = (lane == 0) | (lane == 5) | (lane == 9)
    top = (lane == 1) | (lane == 6) | (lane == 10)
    return jnp.where(low, -1, jnp.where(upper, 16, jnp.where(top, 17, 99)))


def halo_y(lane, j):
    before, behind = (j - 4) % 8, (j - 3) % 8
    choice = (
        ((lane <= 1) | (lane == 15), j),
        (lane == 4, before if before in EDGES else 99),
        ((lane == 5) | (lane == 6), behind if behind in EDGES else 99),
        (lane == 8, EDGES.get(before, 99)),
        ((lane == 9) | (lane == 10), EDGES.get(behind, 99)),
    )
    out = jnp.full(lane.shape, 99, jnp.int32)
    for mask, y in choice:
        out = jnp.where(mask, y, out)
    return out


def domain_tables(cells, fraction_ref):
    cell_x = jnp.right_shift(cells, 7) - 1
    cell_y = jnp.bitwise_and(jnp.right_shift(cells, 4), CY - 1) - 1
    terms_x = spline_terms(fraction_ref[0, 0])
    terms_y = spline_terms(fraction_ref[1, 0])
    lane = row_numbers(16)
    out = banded(lane - cell_x, terms_x) + banded(halo_x(lane) - cell_x, terms_x)
    out += banded(lane - 1 - cell_y, terms_y)
    for j in range(2, 7):
        out += banded(halo_y(lane, j) - cell_y, terms_y)
    return out


def message_blocks(tables):
    wx, dx, wx_halo, dx_halo, wy, dy = tables[:6]

    def row(y):
        return wy[y + 1 : y + 2], dy[y + 1 : y + 2]

    blocks = [(wx, dx) + row(m) for m in range(CY)]
    for j in range(8):
        if j in EDGES:
            blocks.append((wx, dx) + row(EDGES[j]))
        else:
            blocks.append((wx_halo, dx_halo, tables[2 + 2 * j], tables[3 + 2 * j]))
    return blocks


def spread_kernel(
    charge_in, fraction_in, cell_in, live_in, force_in, potential_in, hartley_in,
    send_out, spectral_out, atoms_out,
    charge, fraction, base_cell, live_slot, force_cot, potential_cot, hartley,
    table_a, table_b, table_c, send, spectral, atoms, arrived, left,
):
    pairs = (
        (cell_in, base_cell),
        (fraction_in, fraction),
        (hartley_in, hartley),
        (charge_in, charge),
        (live_in, live_slot),
        (force_in, force_cot),
        (potential_in, potential_cot),
    )
    copies = [
        pltpu.make_async_copy(source, target, arrived.at[index])
        for index, (source, target) in enumerate(pairs)
    ]
    for copy in copies:
        copy.start()
    half = slice(0, 2 * K), slice(2 * K, 4 * K)
    part = slice(0, 2), slice(2, 4)
    results = [
        pltpu.make_async_copy(source, target, left.at[index])
        for index, (source, target) in enumerate((
            (send.at[half[0]], send_out.at[half[0]]),
            (send.at[half[1]], send_out.at[half[1]]),
            (spectral.at[part[0]], spectral_out.at[part[0]]),
            (spectral.at[part[1]], spectral_out.at[part[1]]),
            (atoms, atoms_out),
        ))
    ]

    def store(field, value):
        for row in range(2):
            send[pl.ds(field * 2 * K + row, K, stride=2), :] = value[
                :, row * LANES : (row + 1) * LANES
            ]
        results[field].start()

    def transformed(first, table):
        value = split(product(hart, split(table)))
        spectral[first] = value[0]
        spectral[first + 1] = value[1]
        results[2 + first // 2].start()
        return value

    for copy in copies[0:2]:
        copy.wait()
    cells = base_cell[0]
    slot = lax.broadcasted_iota(jnp.int32, (1, ATOMS), 1)
    base_z = jnp.bitwise_and(slot, -16) + jnp.bitwise_and(cells, 15)
    place_z = jnp.bitwise_and(natural(row_numbers(K)) - (base_z - 1), K - 1)
    wz, dz = banded(place_z, spline_terms(fraction[2, 0]))
    tables = domain_tables(cells, fraction)
    for index, value in enumerate(tables):
        atoms[index * 16 : (index + 1) * 16, :] = value
    for copy in copies[3:]:
        copy.wait()
    live = live_slot[0].astype(jnp.float32)
    live_charge = charge[0] * live
    scalars = (live, live_charge, force_cot[0, 0], force_cot[1, 0], force_cot[2, 0])
    for row, value in enumerate(scalars):
        atoms[SCALARS + row : SCALARS + row + 1, :] = value
    atoms[SCALARS + 5 : SCALARS + 8, :] = jnp.zeros((3, ATOMS), jnp.float32)
    results[4].start()
    along_x = -live_charge * force_cot[0, 0]
    along_y = -live_charge * force_cot[1, 0]
    along_z = -live_charge * force_cot[2, 0]
    direct = live * potential_cot[0]
    for index, (wx, dx, wy, dy) in enumerate(message_blocks(tables)):
        rows = slice(index * 16, (index + 1) * 16)
        table_a[rows, :] = wx * (live_charge * wy)
        table_b[rows, :] = dx * (along_x * wy) + wx * (along_y * dy + direct * wy)
        table_c[rows, :] = wx * (along_z * wy)
    copies[2].wait()
    hart = (hartley[0], hartley[1])
    nt = ((1,), (1,))
    zw = transformed(0, wz)
    store(0, product(zw, split(table_a[...]), nt))
    zd = transformed(2, dz)
    store(1, product(zw, split(table_b[...]), nt) + product(zd, split(table_c[...]), nt))
    for copy in results:
        copy.wait()


def transposed_blocks(values):
    values = list(values)
    block = jnp.right_shift(lax.broadcasted_iota(jnp.int32, values[0].shape, 1), 4)
    for step in (1, 2, 4):
        upper = jnp.bitwise_and(block, step) != 0
        for i in range(8):
            if i & step == 0:
                first, second = values[i], values[i + step]
                values[i] = jnp.where(upper, pltpu.roll(second, 16 * step, 1), first)
                values[i + step] = jnp.where(upper, second, pltpu.roll(first, LANES - 16 * step, 1))
    return values


def plane_kernel(received, hartley, hartley_x, terms, send, plane):
    device = lax.axis_index("gx") * N_GY + lax.axis_index("gy")
    here = lax.broadcasted_iota(jnp.int32, (1, K), 1) == lax.rem(device, K)
    factor_x, square_x, factor_y, square_y = [terms[row : row + 1, :] for row in range(4)]
    factor_z = jnp.sum(jnp.where(here, factor_y, 0.0), axis=1, keepdims=True)
    square_z = jnp.sum(jnp.where(here, square_y, 0.0), axis=1, keepdims=True)
    hy = (hartley[0], hartley[1])
    hx = (hartley_x[0], hartley_x[1])
    place = lax.broadcasted_iota(jnp.int32, (N_GY, LANES), 1)
    block = jnp.right_shift(place, 4)
    lane = jnp.bitwise_and(place, 15)
    low = lane == 15
    high = lane <= 1
    last = block == 7
    first = block <= 1
    edge = last | first

    def rows(gx, half):
        return pl.ds(gx * 2 * N_GY + half, N_GY, stride=2)

    along_x, corners = [], []
    for gx in range(N_GX):
        halo = received[rows(gx, 1), :]
        along_x.append(jnp.where(edge, pltpu.roll(halo, LANES - SHIFT_X, 1), halo))
        corners.append(pltpu.roll(halo, LANES - SHIFT_XY, 1))

    def from_sides(values, gx):
        after, before = values[(gx + 1) % N_GX], values[gx - 1]
        return jnp.where(low, after, jnp.where(high, before, 0.0))

    folded = []
    for gx in range(N_GX):
        own = received[rows(gx, 0), :] + from_sides(along_x, gx)
        side = received[rows(gx, 1), :] + from_sides(corners, gx)
        after, before = pltpu.roll(side, N_GY - 1, 0), pltpu.roll(side, 1, 0)
        folded.append(own + jnp.where(last, after, jnp.where(first, before, 0.0)))
    for group in range(2):
        lines = transposed_blocks(folded[group * 8 : group * 8 + 8])
        for m, line in enumerate(lines):
            plane[m * N_GY : (m + 1) * N_GY, group * LANES : (group + 1) * LANES] = line
    half_way = product(split(plane[...]), hx)
    spectrum = product(hy, split(half_way))
    total_sq = jnp.transpose(square_y) + (square_x + square_z)
    factor = jnp.transpose(factor_y) * (factor_x * (factor_z * (1.0 / (math.pi * K))))
    kernel = jnp.where(total_sq > 0.0, factor / jnp.maximum(total_sq, 1.0), 0.0)
    half_way = product(hy, split(spectrum * kernel))
    plane[...] = product(split(half_way), hx)
    own = []
    for group in range(2):
        own += transposed_blocks(
            plane[m * N_GY : (m + 1) * N_GY, group * LANES : (group + 1) * LANES] for m in range(CY)
        )
    sides = [
        jnp.where(last, pltpu.roll(value, 1, 0), pltpu.roll(value, N_GY - 1, 0)) for value in own
    ]

    def to_sides(values, gx):
        return jnp.where(low, values[gx - 1], values[(gx + 1) % N_GX])

    turned_x = (lane >= 4) & (lane <= 6)
    turned_xy = (lane >= 8) & (lane <= 10)
    for gx in range(N_GX):
        cells_x = to_sides(own, gx)
        cells_xy = to_sides(sides, gx)
        halo = jnp.where(turned_x, pltpu.roll(cells_x, SHIFT_X, 1), cells_x)
        halo = jnp.where(turned_xy, pltpu.roll(cells_xy, SHIFT_XY, 1), halo)
        send[rows(gx, 0), :] = own[gx]
        send[rows(gx, 1), :] = jnp.where(edge, sides[gx], halo)


def sample_kernel(
    received, spectral, atoms, forces, potential, charge_grad, sample_a, sample_b, sample_c
):
    def field(index):
        halves = [received[pl.ds(index * 2 * K + half, K, stride=2), :] for half in range(2)]
        return split(jnp.concatenate(halves, axis=1).T)

    zw = (spectral[0], spectral[1])
    zd = (spectral[2], spectral[3])
    first = field(0)
    sample_a[...] = product(first, zw)
    sample_b[...] = product(first, zd)
    sample_c[...] = product(field(1), zw)
    live, live_charge, along_x, along_y, along_z = [
        atoms[SCALARS + row : SCALARS + row + 1, :] for row in range(5)
    ]
    tables = [atoms[index * 16 : (index + 1) * 16, :] for index in range(16)]
    sums = [jnp.zeros((16, ATOMS), jnp.float32) for _ in range(5)]
    for index, (wx, dx, wy, dy) in enumerate(message_blocks(tables)):
        rows = slice(index * 16, (index + 1) * 16)
        plain = sample_a[rows, :]
        plain_x = wx * plain
        sums[0] = sums[0] + plain_x * wy
        sums[1] = sums[1] + (dx * plain) * wy
        sums[2] = sums[2] + plain_x * dy
        sums[3] = sums[3] + (wx * sample_b[rows, :]) * wy
        sums[4] = sums[4] + (wx * sample_c[rows, :]) * wy
    mesh_value, grad_x, grad_y, grad_z, response = [
        jnp.sum(value, axis=0, keepdims=True) for value in sums
    ]
    forces[0, 0] = -live_charge * grad_x
    forces[1, 0] = -live_charge * grad_y
    forces[2, 0] = -live_charge * grad_z
    potential[0] = live * mesh_value
    charge_grad[0] = live * (response - along_x * grad_x - along_y * grad_y - along_z * grad_z)


def exchange(blocks):
    swapped = lax.all_to_all(
        blocks.reshape(DEVICES, 2, LANES), ("gx", "gy"), split_axis=0, concat_axis=0, tiled=True
    )
    return swapped.reshape(2 * DEVICES, LANES)


def on_device(charge, fraction, base_cell, live_slot, force_cot, potential_cot):
    y = plane_rows()
    freq = np.arange(K)
    hartley = split_table(cas_table(y, y))
    hartley_x = split_table(cas_table(freq, freq))
    factor, square = influence_factors()
    terms = np.zeros((8, K), np.float32)
    terms[:4] = factor, square, factor[y], square[y]
    params = pltpu.CompilerParams(vmem_limit_bytes=48 * 1024 * 1024)
    vmem = pl.BlockSpec(memory_space=pltpu.VMEM)
    hbm = pl.BlockSpec(memory_space=pltpu.HBM)
    f32 = jnp.float32
    table = pltpu.VMEM((K, ATOMS), f32)
    message = jax.ShapeDtypeStruct((2 * DEVICES, LANES), f32)
    arguments = (charge, fraction, base_cell, live_slot, force_cot, potential_cot)

    sent, spectral, atoms = pl.pallas_call(
        spread_kernel,
        out_shape=(
            message,
            jax.ShapeDtypeStruct((4, K, ATOMS), jnp.bfloat16),
            jax.ShapeDtypeStruct((SCALARS + 8, ATOMS), f32),
        ),
        in_specs=[hbm] * 7,
        out_specs=(hbm,) * 3,
        scratch_shapes=[pltpu.VMEM(value.shape, value.dtype) for value in arguments]
        + [pltpu.VMEM(hartley.shape, hartley.dtype), table, table, table]
        + [pltpu.VMEM((2 * DEVICES, LANES), f32), pltpu.VMEM((4, K, ATOMS), jnp.bfloat16)]
        + [pltpu.VMEM((SCALARS + 8, ATOMS), f32), pltpu.SemaphoreType.DMA((7,)), pltpu.SemaphoreType.DMA((5,))],
        compiler_params=pltpu.CompilerParams(vmem_limit_bytes=SPREAD_GRANT),
        name="spread",
    )(*arguments, jnp.asarray(hartley))
    received = exchange(sent)
    solved = pl.pallas_call(
        plane_kernel,
        out_shape=message,
        in_specs=[vmem] * 4,
        out_specs=vmem,
        scratch_shapes=[pltpu.VMEM((K, K), f32)],
        compiler_params=params,
        name="plane",
    )(received, jnp.asarray(hartley), jnp.asarray(hartley_x), jnp.asarray(terms))
    returned = exchange(solved)
    return pl.pallas_call(
        sample_kernel,
        out_shape=(
            jax.ShapeDtypeStruct((3, 1, 1, ATOMS), f32),
            jax.ShapeDtypeStruct((1, 1, ATOMS), f32),
            jax.ShapeDtypeStruct((1, 1, ATOMS), f32),
        ),
        in_specs=[vmem] * 3,
        out_specs=(vmem, vmem, vmem),
        scratch_shapes=[table, table, table],
        compiler_params=params,
        name="sample",
    )(returned, spectral, atoms)


def solution(mesh):
    return jax.shard_map(
        on_device,
        mesh=mesh,
        in_specs=(
            P("gx", "gy", None),
            P(None, "gx", "gy", None),
            P("gx", "gy", None),
            P("gx", "gy", None),
            P(None, "gx", "gy", None),
            P("gx", "gy", None),
        ),
        out_specs=(P(None, "gx", "gy", None), P("gx", "gy", None), P("gx", "gy", None)),
        check_vma=False,
    )
```

time: 83.8 us -> 82.3 us (0.982)
  Pallas kernels: 7.56 us -> 5.97 us
    pallas_call x1, Pallas kernels: 3.26 us -> 2.01 us  [on_device(): pl.pallas_call(plane_kernel, out_shape=message, in_specs=[vmem] * 4, out_...]
where the time goes in v3:
time: 82.3 us; the launch traced here: 82.1 us
  blocking collectives  75.4 us (92%)
  Pallas kernels  5.97 us (7%)
    all_to_all x2, blocking collectives, exchange(): lax.all_to_all(blocks.reshape(DEVICES, 2, LANES), ('gx', 'gy'), split_axi...  75.4 us
    pallas_call x1, Pallas kernels, on_device(): pl.pallas_call(spread_kernel, out_shape=(message, jax.ShapeDtypeStruct((4...  2.84 us
    pallas_call x1, Pallas kernels, on_device(): pl.pallas_call(plane_kernel, out_shape=message, in_specs=[vmem] * 4, out_...  2.01 us

profile of v3, /device:TPU:1, one launch (start us, length us, event | category | flops | bytes accessed | tf_op | source)
XLA Modules:
  0.0 82.1 jit_solution(8926784947276399185)
XLA Ops:
  0.6 2.8 %spread.1 = (f32[1024,128]{1,0:T(8,128)}, bf16[4,256,256]{2,1,0:T(8,128)(2,1)}, f32[264,256]{1,0:T(8,128)}) custom-call(f32[1,1,256]{2,1,0:T(1,128)} %charge_in.1, f32[3,1,1,256]{3,2,1,0:T(1,128)} %fraction_in.1, s32[1,1,256]{2,1,0:T(1,128)} %cell_in.1, s32[1,1,256]{2,1,0:T(1,128)} %live_in.1, f32[3,1,1,256]{3,2,1,0:T(1,128)} %force_in.1, ...), custom_call_target="tpu_custom_call" | custom-call | tf_op jit(solution)/shard_map/spread/pallas_call | solution.py:389
  3.5 0.0 copy-start
  3.5 0.0 copy-start.3
  3.5 0.0 copy-start.4
  3.5 43.7 %all_to_all.10 = f32[512,2,128]{2,1,0:T(2,128)S(1)} all-to-all(f32[512,2,128]{2,1,0:T(2,128)} %bitcast.7), channel_id=1, replica_groups=mesh['gx'=16,'gy'=32] {'gx','gy'}, dimensions={0} | all-to-all | bytes 1048576 | tf_op jit(solution)/shard_map/all_to_all | solution.py:367
  47.2 0.0 copy-done
  47.2 0.0 copy-done.3
  47.2 0.0 copy-done.4
  47.2 2.0 %plane.1 = f32[1024,128]{1,0:T(8,128)S(1)} custom-call(f32[1024,128]{1,0:T(8,128)S(1)} %bitcast.4, bf16[2,256,256]{2,1,0:T(8,128)(2,1)S(1)} %copy-done, bf16[2,256,256]{2,1,0:T(8,128)(2,1)S(1)} %copy-done.3, f32[8,256]{1,0:T(8,128)S(1)} %copy-done.4), custom_call_target="tpu_custom_call" | custom-call | tf_op jit(solution)/shard_map/plane/pallas_call | solution.py:406
  49.3 0.0 copy-start.1
  49.3 0.0 copy-start.2
  49.3 31.7 %all_to_all.11 = f32[512,2,128]{2,1,0:T(2,128)S(1)} all-to-all(f32[512,2,128]{2,1,0:T(2,128)S(1)} %bitcast.5), channel_id=1, replica_groups=mesh['gx'=16,'gy'=32] {'gx','gy'}, dimensions={0} | all-to-all | bytes 1048576 | tf_op jit(solution)/shard_map/all_to_all | solution.py:367
  80.9 0.0 copy-done.1
  80.9 0.0 copy-done.2
  80.9 1.1 %sample.1 = (f32[3,1,1,256]{3,2,1,0:T(1,128)}, f32[1,1,256]{2,1,0:T(1,128)}, f32[1,1,256]{2,1,0:T(1,128)}) custom-call(f32[1024,128]{1,0:T(8,128)S(1)} %bitcast.6, bf16[4,256,256]{2,1,0:T(8,128)(2,1)S(1)} %copy-done.1, f32[264,256]{1,0:T(8,128)S(1)} %copy-done.2), custom_call_target="tpu_custom_call" | custom-call | tf_op jit(solution)/shard_map/sample/pallas_call | solution.py:416
Async XLA Ops:
  3.5 43.8 %copy-start = (bf16[2,256,256]{2,1,0:T(8,128)(2,1)S(1)}, bf16[2,256,256]{2,1,0:T(8,128)(2,1)}, u32[]{:S(2)}) copy-start(bf16[2,256,256]{2,1,0:T(8,128)(2,1)} %constant.6.clone.hartley_in.hartley) | copy-start | bytes 786436
  3.5 43.8 %copy-start.3 = (bf16[2,256,256]{2,1,0:T(8,128)(2,1)S(1)}, bf16[2,256,256]{2,1,0:T(8,128)(2,1)}, u32[]{:S(2)}) copy-start(bf16[2,256,256]{2,1,0:T(8,128)(2,1)} %constant.7.clone.hartley_x) | copy-start | bytes 786436
  3.5 43.7 %copy-start.4 = (f32[8,256]{1,0:T(8,128)S(1)}, f32[8,256]{1,0:T(8,128)}, u32[]{:S(2)}) copy-start(f32[8,256]{1,0:T(8,128)} %constant.8.clone.terms) | copy-start | bytes 24580
  49.3 31.7 %copy-start.1 = (bf16[4,256,256]{2,1,0:T(8,128)(2,1)S(1)}, bf16[4,256,256]{2,1,0:T(8,128)(2,1)}, u32[]{:S(2)}) copy-start(bf16[4,256,256]{2,1,0:T(8,128)(2,1)} %get-tuple-element.7.spectral) | copy-start | bytes 1572868
  49.3 31.7 %copy-start.2 = (f32[264,256]{1,0:T(8,128)S(1)}, f32[264,256]{1,0:T(8,128)}, u32[]{:S(2)}) copy-start(f32[264,256]{1,0:T(8,128)} %get-tuple-element.8.atoms) | copy-start | bytes 811012

commit v4 on v3

--- a/solution.py
+++ b/solution.py
@@ -17,7 +17,6 @@
 DEVICES = N_GX * N_GY
 LANES = 128
 SCALARS = 256
-SPREAD_GRANT = 60 * 1024 * 1024
 
 EWALD_SPLIT = 0.8
 
@@ -156,73 +155,40 @@
     return blocks
 
 
+def rows_kernel(rows):
+    rows[...] = natural(row_numbers(K))
+
+
 def spread_kernel(
-    charge_in, fraction_in, cell_in, live_in, force_in, potential_in, hartley_in,
-    send_out, spectral_out, atoms_out,
-    charge, fraction, base_cell, live_slot, force_cot, potential_cot, hartley,
-    table_a, table_b, table_c, send, spectral, atoms, arrived, left,
+    rows, charge, fraction, base_cell, live_slot, force_cot, potential_cot, hartley,
+    send, spectral, atoms, table_a, table_b, table_c,
 ):
-    pairs = (
-        (cell_in, base_cell),
-        (fraction_in, fraction),
-        (hartley_in, hartley),
-        (charge_in, charge),
-        (live_in, live_slot),
-        (force_in, force_cot),
-        (potential_in, potential_cot),
-    )
-    copies = [
-        pltpu.make_async_copy(source, target, arrived.at[index])
-        for index, (source, target) in enumerate(pairs)
-    ]
-    for copy in copies:
-        copy.start()
-    half = slice(0, 2 * K), slice(2 * K, 4 * K)
-    part = slice(0, 2), slice(2, 4)
-    results = [
-        pltpu.make_async_copy(source, target, left.at[index])
-        for index, (source, target) in enumerate((
-            (send.at[half[0]], send_out.at[half[0]]),
-            (send.at[half[1]], send_out.at[half[1]]),
-            (spectral.at[part[0]], spectral_out.at[part[0]]),
-            (spectral.at[part[1]], spectral_out.at[part[1]]),
-            (atoms, atoms_out),
-        ))
-    ]
-
     def store(field, value):
         for row in range(2):
             send[pl.ds(field * 2 * K + row, K, stride=2), :] = value[
                 :, row * LANES : (row + 1) * LANES
             ]
-        results[field].start()
 
     def transformed(first, table):
         value = split(product(hart, split(table)))
         spectral[first] = value[0]
         spectral[first + 1] = value[1]
-        results[2 + first // 2].start()
         return value
 
-    for copy in copies[0:2]:
-        copy.wait()
     cells = base_cell[0]
     slot = lax.broadcasted_iota(jnp.int32, (1, ATOMS), 1)
     base_z = jnp.bitwise_and(slot, -16) + jnp.bitwise_and(cells, 15)
-    place_z = jnp.bitwise_and(natural(row_numbers(K)) - (base_z - 1), K - 1)
+    place_z = jnp.bitwise_and(rows[...] - (base_z - 1), K - 1)
     wz, dz = banded(place_z, spline_terms(fraction[2, 0]))
     tables = domain_tables(cells, fraction)
     for index, value in enumerate(tables):
         atoms[index * 16 : (index + 1) * 16, :] = value
-    for copy in copies[3:]:
-        copy.wait()
     live = live_slot[0].astype(jnp.float32)
     live_charge = charge[0] * live
     scalars = (live, live_charge, force_cot[0, 0], force_cot[1, 0], force_cot[2, 0])
     for row, value in enumerate(scalars):
         atoms[SCALARS + row : SCALARS + row + 1, :] = value
     atoms[SCALARS + 5 : SCALARS + 8, :] = jnp.zeros((3, ATOMS), jnp.float32)
-    results[4].start()
     along_x = -live_charge * force_cot[0, 0]
     along_y = -live_charge * force_cot[1, 0]
     along_z = -live_charge * force_cot[2, 0]
@@ -232,15 +198,12 @@
         table_a[rows, :] = wx * (live_charge * wy)
         table_b[rows, :] = dx * (along_x * wy) + wx * (along_y * dy + direct * wy)
         table_c[rows, :] = wx * (along_z * wy)
-    copies[2].wait()
     hart = (hartley[0], hartley[1])
     nt = ((1,), (1,))
     zw = transformed(0, wz)
     store(0, product(zw, split(table_a[...]), nt))
     zd = transformed(2, dz)
     store(1, product(zw, split(table_b[...]), nt) + product(zd, split(table_c[...]), nt))
-    for copy in results:
-        copy.wait()
 
 
 def transposed_blocks(values):
@@ -378,14 +341,21 @@
     factor, square = influence_factors()
     terms = np.zeros((8, K), np.float32)
     terms[:4] = factor, square, factor[y], square[y]
-    params = pltpu.CompilerParams(vmem_limit_bytes=48 * 1024 * 1024)
+    params = pltpu.CompilerParams(vmem_limit_bytes=32 * 1024 * 1024)
     vmem = pl.BlockSpec(memory_space=pltpu.VMEM)
-    hbm = pl.BlockSpec(memory_space=pltpu.HBM)
     f32 = jnp.float32
     table = pltpu.VMEM((K, ATOMS), f32)
     message = jax.ShapeDtypeStruct((2 * DEVICES, LANES), f32)
     arguments = (charge, fraction, base_cell, live_slot, force_cot, potential_cot)
 
+    rows = pl.pallas_call(
+        rows_kernel,
+        out_shape=jax.ShapeDtypeStruct((K, ATOMS), jnp.int32),
+        out_specs=vmem,
+        compiler_params=params,
+        cost_estimate=pl.CostEstimate(flops=10**9, bytes_accessed=10**6, transcendentals=0),
+        name="rows",
+    )()
     sent, spectral, atoms = pl.pallas_call(
         spread_kernel,
         out_shape=(
@@ -393,15 +363,12 @@
             jax.ShapeDtypeStruct((4, K, ATOMS), jnp.bfloat16),
             jax.ShapeDtypeStruct((SCALARS + 8, ATOMS), f32),
         ),
-        in_specs=[hbm] * 7,
-        out_specs=(hbm,) * 3,
-        scratch_shapes=[pltpu.VMEM(value.shape, value.dtype) for value in arguments]
-        + [pltpu.VMEM(hartley.shape, hartley.dtype), table, table, table]
-        + [pltpu.VMEM((2 * DEVICES, LANES), f32), pltpu.VMEM((4, K, ATOMS), jnp.bfloat16)]
-        + [pltpu.VMEM((SCALARS + 8, ATOMS), f32), pltpu.SemaphoreType.DMA((7,)), pltpu.SemaphoreType.DMA((5,))],
-        compiler_params=pltpu.CompilerParams(vmem_limit_bytes=SPREAD_GRANT),
+        in_specs=[vmem] * 8,
+        out_specs=(vmem,) * 3,
+        scratch_shapes=[table, table, table],
+        compiler_params=params,
         name="spread",
-    )(*arguments, jnp.asarray(hartley))
+    )(rows, *arguments, jnp.asarray(hartley))
     received = exchange(sent)
     solved = pl.pallas_call(
         plane_kernel,

time: 82.3 us -> 81 us (0.984)
  Pallas kernels: 5.97 us -> 4.21 us
  local copies, waits for them, and re-layouts: 0.03 us -> 0.89 us
    pallas_call x1, Pallas kernels: 2.84 us -> 1.05 us  [on_device(): pl.pallas_call(spread_kernel, out_shape=(message, jax.ShapeDtypeStruct((4...]
    unnamed x10 -> x18, local copies, waits for them, and re-layouts: 0.03 us -> 0.89 us
where the time goes in v4:
time: 81 us; the launch traced here: 80.9 us
  blocking collectives  75 us (93%)
  Pallas kernels  4.21 us (5%)
  local copies, waits for them, and re-layouts  0.89 us (1%)
    all_to_all x2, blocking collectives, exchange(): lax.all_to_all(blocks.reshape(DEVICES, 2, LANES), ('gx', 'gy'), split_axi...  75 us
    pallas_call x1, Pallas kernels, on_device(): pl.pallas_call(plane_kernel, out_shape=message, in_specs=[vmem] * 4, out_...  2.01 us

profile of v4, /device:TPU:1, one launch (start us, length us, event | category | flops | bytes accessed | tf_op | source)
XLA Modules:
  0.0 80.9 jit_solution(12663386888815978484)
XLA Ops:
  0.6 0.0 copy-start
  0.6 0.0 copy-start.8
  0.7 0.0 copy-start.4
  0.7 0.0 copy-start.7
  0.7 0.0 copy-start.6
  0.7 0.0 copy-start.3
  0.7 0.0 copy-start.5
  0.7 0.8 %copy-done = bf16[2,256,256]{2,1,0:T(8,128)(2,1)S(1)} copy-done((bf16[2,256,256]{2,1,0:T(8,128)(2,1)S(1)}, bf16[2,256,256]{2,1,0:T(8,128)(2,1)}, u32[]{:S(2)}) %copy-start) | copy-done | bytes 262168
  1.6 0.0 copy-done.8
  1.6 0.0 copy-done.4
  1.6 0.0 copy-done.7
  1.6 0.0 copy-done.6
  1.6 0.0 copy-done.3
  1.6 0.0 copy-done.5
  1.6 1.0 %spread.1 = (f32[1024,128]{1,0:T(8,128)S(1)}, bf16[4,256,256]{2,1,0:T(8,128)(2,1)S(1)}, f32[264,256]{1,0:T(8,128)S(1)}) custom-call(s32[256,256]{1,0:T(8,128)S(1)} %rows.1, f32[1,1,256]{2,1,0:T(1,128)S(1)} %copy-done.5, f32[3,1,1,256]{3,2,1,0:T(1,128)S(1)} %copy-done.3, s32[1,1,256]{2,1,0:T(1,128)S(1)} %copy-done.6, s32[1,1,256]{2,1,0:T(1,128)S(1)} %copy-done.7, ...), custom_call_target="tpu_custom_call" | custom-call | tf_op jit(solution)/shard_map/spread/pallas_call | solution.py:359
  2.7 0.0 copy-start.1
  2.7 0.0 copy-start.2
  2.7 43.5 %all_to_all.10 = f32[512,2,128]{2,1,0:T(2,128)S(1)} all-to-all(f32[512,2,128]{2,1,0:T(2,128)S(1)} %bitcast.7), channel_id=1, replica_groups=mesh['gx'=16,'gy'=32] {'gx','gy'}, dimensions={0} | all-to-all | bytes 1048576 | tf_op jit(solution)/shard_map/all_to_all | solution.py:330
  46.2 0.0 copy-done.1
  46.2 0.0 copy-done.2
  46.2 2.0 %plane.1 = f32[1024,128]{1,0:T(8,128)S(1)} custom-call(f32[1024,128]{1,0:T(8,128)S(1)} %bitcast.4, bf16[2,256,256]{2,1,0:T(8,128)(2,1)S(1)} %copy-done, bf16[2,256,256]{2,1,0:T(8,128)(2,1)S(1)} %copy-done.1, f32[8,256]{1,0:T(8,128)S(1)} %copy-done.2), custom_call_target="tpu_custom_call" | custom-call | tf_op jit(solution)/shard_map/plane/pallas_call | solution.py:373
  48.2 31.5 %all_to_all.11 = f32[512,2,128]{2,1,0:T(2,128)S(1)} all-to-all(f32[512,2,128]{2,1,0:T(2,128)S(1)} %bitcast.5), channel_id=1, replica_groups=mesh['gx'=16,'gy'=32] {'gx','gy'}, dimensions={0} | all-to-all | bytes 1048576 | tf_op jit(solution)/shard_map/all_to_all | solution.py:330
  79.7 1.1 %sample.1 = (f32[3,1,1,256]{3,2,1,0:T(1,128)}, f32[1,1,256]{2,1,0:T(1,128)}, f32[1,1,256]{2,1,0:T(1,128)}) custom-call(f32[1024,128]{1,0:T(8,128)S(1)} %bitcast.6, bf16[4,256,256]{2,1,0:T(8,128)(2,1)S(1)} %get-tuple-element.7.spectral, f32[264,256]{1,0:T(8,128)S(1)} %get-tuple-element.8.atoms), custom_call_target="tpu_custom_call" | custom-call | tf_op jit(solution)/shard_map/sample/pallas_call | solution.py:383
  (1 shorter events, 0.0 us)
Async XLA Ops:
  0.6 1.0 %copy-start = (bf16[2,256,256]{2,1,0:T(8,128)(2,1)S(1)}, bf16[2,256,256]{2,1,0:T(8,128)(2,1)}, u32[]{:S(2)}) copy-start(bf16[2,256,256]{2,1,0:T(8,128)(2,1)} %constant.6.clone.hartley) | copy-start | bytes 786436
  0.6 0.9 %copy-start.8 = (f32[1,1,256]{2,1,0:T(1,128)S(1)}, f32[1,1,256]{2,1,0:T(1,128)}, u32[]{:S(2)}) copy-start(f32[1,1,256]{2,1,0:T(1,128)} %potential_cot.1) | copy-start | bytes 3076
  0.7 0.9 %copy-start.4 = (f32[3,1,1,256]{3,2,1,0:T(1,128)S(1)}, f32[3,1,1,256]{3,2,1,0:T(1,128)}, u32[]{:S(2)}) copy-start(f32[3,1,1,256]{3,2,1,0:T(1,128)} %force_cot.1) | copy-start | bytes 9220
  0.7 0.9 %copy-start.7 = (s32[1,1,256]{2,1,0:T(1,128)S(1)}, s32[1,1,256]{2,1,0:T(1,128)}, u32[]{:S(2)}) copy-start(s32[1,1,256]{2,1,0:T(1,128)} %live_slot.1) | copy-start | bytes 3076
  0.7 0.9 %copy-start.6 = (s32[1,1,256]{2,1,0:T(1,128)S(1)}, s32[1,1,256]{2,1,0:T(1,128)}, u32[]{:S(2)}) copy-start(s32[1,1,256]{2,1,0:T(1,128)} %base_cell.1) | copy-start | bytes 3076
  0.7 0.9 %copy-start.3 = (f32[3,1,1,256]{3,2,1,0:T(1,128)S(1)}, f32[3,1,1,256]{3,2,1,0:T(1,128)}, u32[]{:S(2)}) copy-start(f32[3,1,1,256]{3,2,1,0:T(1,128)} %fraction.1) | copy-start | bytes 9220
  0.7 0.9 %copy-start.5 = (f32[1,1,256]{2,1,0:T(1,128)S(1)}, f32[1,1,256]{2,1,0:T(1,128)}, u32[]{:S(2)}) copy-start(f32[1,1,256]{2,1,0:T(1,128)} %charge.1) | copy-start | bytes 3076
  2.7 43.5 %copy-start.1 = (bf16[2,256,256]{2,1,0:T(8,128)(2,1)S(1)}, bf16[2,256,256]{2,1,0:T(8,128)(2,1)}, u32[]{:S(2)}) copy-start(bf16[2,256,256]{2,1,0:T(8,128)(2,1)} %constant.7.clone.hartley_x) | copy-start | bytes 786436
  2.7 43.5 %copy-start.2 = (f32[8,256]{1,0:T(8,128)S(1)}, f32[8,256]{1,0:T(8,128)}, u32[]{:S(2)}) copy-start(f32[8,256]{1,0:T(8,128)} %constant.8.clone.terms) | copy-start | bytes 24580

commit v5 on v4

--- a/solution.py
+++ b/solution.py
@@ -157,6 +157,21 @@
 
 def rows_kernel(rows):
     rows[...] = natural(row_numbers(K))
+
+
+def table_kernel(rows, hartley):
+    cell = rows[...]
+    frequency = natural(lax.broadcasted_iota(jnp.int32, (K, K), 1))
+    turn = jnp.bitwise_and(cell * frequency + K // 8, K - 1) - K // 2
+    quarter = jnp.where(turn > K // 4, K // 2 - turn, jnp.where(turn < -K // 4, -K // 2 - turn, turn))
+    angle = quarter.astype(jnp.float32) * (2.0 * math.pi / K)
+    square = angle * angle
+    series = jnp.full((K, K), -1.0 / math.factorial(11), jnp.float32)
+    for order in (9, 7, 5, 3, 1):
+        series = series * square + (-1.0) ** (order // 2) / math.factorial(order)
+    high, low = split(series * angle * -math.sqrt(2.0))
+    hartley[0] = high
+    hartley[1] = low
 
 
 def spread_kernel(
@@ -201,8 +216,8 @@
     hart = (hartley[0], hartley[1])
     nt = ((1,), (1,))
     zw = transformed(0, wz)
+    zd = transformed(2, dz)
     store(0, product(zw, split(table_a[...]), nt))
-    zd = transformed(2, dz)
     store(1, product(zw, split(table_b[...]), nt) + product(zd, split(table_c[...]), nt))
 
 
@@ -336,7 +351,6 @@
 def on_device(charge, fraction, base_cell, live_slot, force_cot, potential_cot):
     y = plane_rows()
     freq = np.arange(K)
-    hartley = split_table(cas_table(y, y))
     hartley_x = split_table(cas_table(freq, freq))
     factor, square = influence_factors()
     terms = np.zeros((8, K), np.float32)
@@ -356,6 +370,15 @@
         cost_estimate=pl.CostEstimate(flops=10**9, bytes_accessed=10**6, transcendentals=0),
         name="rows",
     )()
+    hartley = pl.pallas_call(
+        table_kernel,
+        out_shape=jax.ShapeDtypeStruct((2, K, K), jnp.bfloat16),
+        in_specs=[vmem],
+        out_specs=vmem,
+        compiler_params=params,
+        cost_estimate=pl.CostEstimate(flops=10**9, bytes_accessed=10**6, transcendentals=0),
+        name="tables",
+    )(rows)
     sent, spectral, atoms = pl.pallas_call(
         spread_kernel,
         out_shape=(
@@ -368,7 +391,7 @@
         scratch_shapes=[table, table, table],
         compiler_params=params,
         name="spread",
-    )(rows, *arguments, jnp.asarray(hartley))
+    )(rows, *arguments, hartley)
     received = exchange(sent)
     solved = pl.pallas_call(
         plane_kernel,
@@ -378,7 +401,7 @@
         scratch_shapes=[pltpu.VMEM((K, K), f32)],
         compiler_params=params,
         name="plane",
-    )(received, jnp.asarray(hartley), jnp.asarray(hartley_x), jnp.asarray(terms))
+    )(received, hartley, jnp.asarray(hartley_x), jnp.asarray(terms))
     returned = exchange(solved)
     return pl.pallas_call(
         sample_kernel,

time: 81 us -> 80.8 us (level)
  no operation moved by 1% of the time
where the time goes in v5:
time: 80.8 us; the launch traced here: 80.6 us
  blocking collectives  75 us (93%)
  Pallas kernels  4.39 us (5%)
    all_to_all x2, blocking collectives, exchange(): lax.all_to_all(blocks.reshape(DEVICES, 2, LANES), ('gx', 'gy'), split_axi...  75 us
    pallas_call x1, Pallas kernels, on_device(): pl.pallas_call(plane_kernel, out_shape=message, in_specs=[vmem] * 4, out_...  2.01 us

profile of v5, /device:TPU:1, one launch (start us, length us, event | category | flops | bytes accessed | tf_op | source)
XLA Modules:
  0.0 80.6 jit_solution(15401805932463964491)
XLA Ops:
  0.7 0.0 copy-start.2
  0.7 0.0 copy-start.3
  0.7 0.0 copy-start.4
  0.7 0.0 copy-start.5
  0.7 0.0 copy-start.6
  0.7 0.0 copy-start.7
  0.7 0.3 tables.1.hartley
  1.0 0.3 copy-done.2
  1.4 0.0 copy-done.3
  1.4 0.0 copy-done.4
  1.4 0.0 copy-done.5
  1.4 0.0 copy-done.6
  1.4 0.0 copy-done.7
  1.4 1.0 %spread.1 = (f32[1024,128]{1,0:T(8,128)S(1)}, bf16[4,256,256]{2,1,0:T(8,128)(2,1)S(1)}, f32[264,256]{1,0:T(8,128)S(1)}) custom-call(s32[256,256]{1,0:T(8,128)S(1)} %rows.1, f32[1,1,256]{2,1,0:T(1,128)S(1)} %copy-done.4, f32[3,1,1,256]{3,2,1,0:T(1,128)S(1)} %copy-done.2, s32[1,1,256]{2,1,0:T(1,128)S(1)} %copy-done.5, s32[1,1,256]{2,1,0:T(1,128)S(1)} %copy-done.6, ...), custom_call_target="tpu_custom_call" | custom-call | tf_op jit(solution)/shard_map/spread/pallas_call | solution.py:382
  2.4 0.0 copy-start
  2.4 0.0 copy-start.1
  2.4 43.5 %all_to_all.10 = f32[512,2,128]{2,1,0:T(2,128)S(1)} all-to-all(f32[512,2,128]{2,1,0:T(2,128)S(1)} %bitcast.7), channel_id=1, replica_groups=mesh['gx'=16,'gy'=32] {'gx','gy'}, dimensions={0} | all-to-all | bytes 1048576 | tf_op jit(solution)/shard_map/all_to_all | solution.py:345
  45.9 0.0 copy-done
  45.9 0.0 copy-done.1
  45.9 2.0 %plane.1 = f32[1024,128]{1,0:T(8,128)S(1)} custom-call(f32[1024,128]{1,0:T(8,128)S(1)} %bitcast.4, bf16[2,256,256]{2,1,0:T(8,128)(2,1)S(1)} %tables.1.hartley, bf16[2,256,256]{2,1,0:T(8,128)(2,1)S(1)} %copy-done, f32[8,256]{1,0:T(8,128)S(1)} %copy-done.1), custom_call_target="tpu_custom_call" | custom-call | tf_op jit(solution)/shard_map/plane/pallas_call | solution.py:396
  47.9 31.5 %all_to_all.11 = f32[512,2,128]{2,1,0:T(2,128)S(1)} all-to-all(f32[512,2,128]{2,1,0:T(2,128)S(1)} %bitcast.5), channel_id=1, replica_groups=mesh['gx'=16,'gy'=32] {'gx','gy'}, dimensions={0} | all-to-all | bytes 1048576 | tf_op jit(solution)/shard_map/all_to_all | solution.py:345
  79.5 1.1 %sample.1 = (f32[3,1,1,256]{3,2,1,0:T(1,128)}, f32[1,1,256]{2,1,0:T(1,128)}, f32[1,1,256]{2,1,0:T(1,128)}) custom-call(f32[1024,128]{1,0:T(8,128)S(1)} %bitcast.6, bf16[4,256,256]{2,1,0:T(8,128)(2,1)S(1)} %get-tuple-element.7.spectral, f32[264,256]{1,0:T(8,128)S(1)} %get-tuple-element.8.atoms), custom_call_target="tpu_custom_call" | custom-call | tf_op jit(solution)/shard_map/sample/pallas_call | solution.py:406
  (1 shorter events, 0.0 us)
Async XLA Ops:
  0.7 0.7 copy-start.2
  0.7 0.7 copy-start.3
  0.7 0.7 copy-start.4
  0.7 0.7 copy-start.5
  0.7 0.7 copy-start.6
  0.7 0.7 copy-start.7
  2.4 43.5 %copy-start = (bf16[2,256,256]{2,1,0:T(8,128)(2,1)S(1)}, bf16[2,256,256]{2,1,0:T(8,128)(2,1)}, u32[]{:S(2)}) copy-start(bf16[2,256,256]{2,1,0:T(8,128)(2,1)} %constant.4.clone.hartley_x) | copy-start | bytes 786436
  2.4 43.5 %copy-start.1 = (f32[8,256]{1,0:T(8,128)S(1)}, f32[8,256]{1,0:T(8,128)}, u32[]{:S(2)}) copy-start(f32[8,256]{1,0:T(8,128)} %constant.5.clone.terms) | copy-start | bytes 24580

commit v6 on v5

--- a/solution.py
+++ b/solution.py
@@ -234,13 +234,12 @@
     return values
 
 
-def plane_kernel(received, hartley, hartley_x, terms, send, plane):
+def plane_kernel(received, hartley, hartley_x, terms, send):
     device = lax.axis_index("gx") * N_GY + lax.axis_index("gy")
     here = lax.broadcasted_iota(jnp.int32, (1, K), 1) == lax.rem(device, K)
     factor_x, square_x, factor_y, square_y = [terms[row : row + 1, :] for row in range(4)]
     factor_z = jnp.sum(jnp.where(here, factor_y, 0.0), axis=1, keepdims=True)
     square_z = jnp.sum(jnp.where(here, square_y, 0.0), axis=1, keepdims=True)
-    hy = (hartley[0], hartley[1])
     hx = (hartley_x[0], hartley_x[1])
     place = lax.broadcasted_iota(jnp.int32, (N_GY, LANES), 1)
     block = jnp.right_shift(place, 4)
@@ -270,21 +269,30 @@
         side = received[rows(gx, 1), :] + from_sides(corners, gx)
         after, before = pltpu.roll(side, N_GY - 1, 0), pltpu.roll(side, 1, 0)
         folded.append(own + jnp.where(last, after, jnp.where(first, before, 0.0)))
-    for group in range(2):
-        lines = transposed_blocks(folded[group * 8 : group * 8 + 8])
-        for m, line in enumerate(lines):
-            plane[m * N_GY : (m + 1) * N_GY, group * LANES : (group + 1) * LANES] = line
-    half_way = product(split(plane[...]), hx)
-    spectrum = product(hy, split(half_way))
+    groups = [transposed_blocks(folded[group * 8 : group * 8 + 8]) for group in range(2)]
     total_sq = jnp.transpose(square_y) + (square_x + square_z)
     factor = jnp.transpose(factor_y) * (factor_x * (factor_z * (1.0 / (math.pi * K))))
     kernel = jnp.where(total_sq > 0.0, factor / jnp.maximum(total_sq, 1.0), 0.0)
-    half_way = product(hy, split(spectrum * kernel))
-    plane[...] = product(split(half_way), hx)
+    cuts = slice(0, K // 2), slice(K // 2, K)
+    hy = [(hartley[0, cut, :], hartley[1, cut, :]) for cut in cuts]
+
+    def joined(blocks):
+        return tuple(jnp.concatenate(pair, axis=0) for pair in zip(*blocks))
+
+    lines = [
+        jnp.concatenate([jnp.concatenate(group[m : m + 4], axis=0) for group in groups], axis=1)
+        for m in (0, 4)
+    ]
+    half_way = joined([split(product(split(line), hx)) for line in lines])
+    spectrum = [product(block, half_way) * kernel[cut] for block, cut in zip(hy, cuts)]
+    spectrum = joined([split(block) for block in spectrum])
+    half_way = [product(block, spectrum) for block in hy]
+    solved = [product(split(block), hx) for block in half_way]
     own = []
     for group in range(2):
+        lanes = slice(group * LANES, (group + 1) * LANES)
         own += transposed_blocks(
-            plane[m * N_GY : (m + 1) * N_GY, group * LANES : (group + 1) * LANES] for m in range(CY)
+            solved[m // 4][m % 4 * N_GY : (m % 4 + 1) * N_GY, lanes] for m in range(CY)
         )
     sides = [
         jnp.where(last, pltpu.roll(value, 1, 0), pltpu.roll(value, N_GY - 1, 0)) for value in own
@@ -398,7 +406,6 @@
         out_shape=message,
         in_specs=[vmem] * 4,
         out_specs=vmem,
-        scratch_shapes=[pltpu.VMEM((K, K), f32)],
         compiler_params=params,
         name="plane",
     )(received, hartley, jnp.asarray(hartley_x), jnp.asarray(terms))

time: 80.8 us -> 80.6 us (level)
  no operation moved by 1% of the time
where the time goes in v6:
time: 80.6 us; the launch traced here: 80.4 us
  blocking collectives  75 us (93%)
  Pallas kernels  4.2 us (5%)
    all_to_all x2, blocking collectives, exchange(): lax.all_to_all(blocks.reshape(DEVICES, 2, LANES), ('gx', 'gy'), split_axi...  75 us
    pallas_call x1, Pallas kernels, on_device(): pl.pallas_call(plane_kernel, out_shape=message, in_specs=[vmem] * 4, out_...  1.83 us

profile of v6, /device:TPU:1, one launch (start us, length us, event | category | flops | bytes accessed | tf_op | source)
XLA Modules:
  0.0 80.4 jit_solution(16870963555267667756)
XLA Ops:
  0.7 0.0 copy-start.2
  0.7 0.0 copy-start.3
  0.7 0.0 copy-start.4
  0.7 0.0 copy-start.5
  0.7 0.0 copy-start.6
  0.7 0.0 copy-start.7
  0.7 0.3 tables.1.hartley
  1.0 0.3 copy-done.2
  1.4 0.0 copy-done.3
  1.4 0.0 copy-done.4
  1.4 0.0 copy-done.5
  1.4 0.0 copy-done.6
  1.4 0.0 copy-done.7
  1.4 1.0 %spread.1 = (f32[1024,128]{1,0:T(8,128)S(1)}, bf16[4,256,256]{2,1,0:T(8,128)(2,1)S(1)}, f32[264,256]{1,0:T(8,128)S(1)}) custom-call(s32[256,256]{1,0:T(8,128)S(1)} %rows.1, f32[1,1,256]{2,1,0:T(1,128)S(1)} %copy-done.4, f32[3,1,1,256]{3,2,1,0:T(1,128)S(1)} %copy-done.2, s32[1,1,256]{2,1,0:T(1,128)S(1)} %copy-done.5, s32[1,1,256]{2,1,0:T(1,128)S(1)} %copy-done.6, ...), custom_call_target="tpu_custom_call" | custom-call | tf_op jit(solution)/shard_map/spread/pallas_call | solution.py:390
  2.4 0.0 copy-start
  2.4 0.0 copy-start.1
  2.4 43.5 %all_to_all.10 = f32[512,2,128]{2,1,0:T(2,128)S(1)} all-to-all(f32[512,2,128]{2,1,0:T(2,128)S(1)} %bitcast.7), channel_id=1, replica_groups=mesh['gx'=16,'gy'=32] {'gx','gy'}, dimensions={0} | all-to-all | bytes 1048576 | tf_op jit(solution)/shard_map/all_to_all | solution.py:353
  45.9 0.0 copy-done
  45.9 0.0 copy-done.1
  45.9 1.8 %plane.1 = f32[1024,128]{1,0:T(8,128)S(1)} custom-call(f32[1024,128]{1,0:T(8,128)S(1)} %bitcast.4, bf16[2,256,256]{2,1,0:T(8,128)(2,1)S(1)} %tables.1.hartley, bf16[2,256,256]{2,1,0:T(8,128)(2,1)S(1)} %copy-done, f32[8,256]{1,0:T(8,128)S(1)} %copy-done.1), custom_call_target="tpu_custom_call" | custom-call | tf_op jit(solution)/shard_map/plane/pallas_call | solution.py:404
  47.8 31.5 %all_to_all.11 = f32[512,2,128]{2,1,0:T(2,128)S(1)} all-to-all(f32[512,2,128]{2,1,0:T(2,128)S(1)} %bitcast.5), channel_id=1, replica_groups=mesh['gx'=16,'gy'=32] {'gx','gy'}, dimensions={0} | all-to-all | bytes 1048576 | tf_op jit(solution)/shard_map/all_to_all | solution.py:353
  79.3 1.1 %sample.1 = (f32[3,1,1,256]{3,2,1,0:T(1,128)}, f32[1,1,256]{2,1,0:T(1,128)}, f32[1,1,256]{2,1,0:T(1,128)}) custom-call(f32[1024,128]{1,0:T(8,128)S(1)} %bitcast.6, bf16[4,256,256]{2,1,0:T(8,128)(2,1)S(1)} %get-tuple-element.7.spectral, f32[264,256]{1,0:T(8,128)S(1)} %get-tuple-element.8.atoms), custom_call_target="tpu_custom_call" | custom-call | tf_op jit(solution)/shard_map/sample/pallas_call | solution.py:413
  (1 shorter events, 0.0 us)
Async XLA Ops:
  0.7 0.7 copy-start.2
  0.7 0.7 copy-start.3
  0.7 0.7 copy-start.4
  0.7 0.7 copy-start.5
  0.7 0.7 copy-start.6
  0.7 0.7 copy-start.7
  2.4 43.5 %copy-start = (bf16[2,256,256]{2,1,0:T(8,128)(2,1)S(1)}, bf16[2,256,256]{2,1,0:T(8,128)(2,1)}, u32[]{:S(2)}) copy-start(bf16[2,256,256]{2,1,0:T(8,128)(2,1)} %constant.4.clone.hartley_x) | copy-start | bytes 786436
  2.4 43.5 %copy-start.1 = (f32[8,256]{1,0:T(8,128)S(1)}, f32[8,256]{1,0:T(8,128)}, u32[]{:S(2)}) copy-start(f32[8,256]{1,0:T(8,128)} %constant.5.clone.terms) | copy-start | bytes 24580

commit v7 on v6

--- a/solution.py
+++ b/solution.py
@@ -17,6 +17,7 @@
 DEVICES = N_GX * N_GY
 LANES = 128
 SCALARS = 256
+HALVES = (slice(0, K // 2), slice(K // 2, K))
 
 EWALD_SPLIT = 0.8
 
@@ -63,6 +64,10 @@
         return lax.dot_general(a, b, (dims, ((), ())), preferred_element_type=jnp.float32)
 
     return one(left[0], right[0]) + (one(left[0], right[1]) + one(left[1], right[0]))
+
+
+def joined(blocks):
+    return tuple(jnp.concatenate(pair, axis=0) for pair in zip(*blocks))
 
 
 def spline_terms(fraction):
@@ -174,6 +179,27 @@
     hartley[1] = low
 
 
+def z_tables(rows, first, terms):
+    zeros = [jnp.zeros((8, LANES), jnp.float32)] * 2
+    halves = []
+    for half in range(2):
+        lanes = slice(half * LANES, (half + 1) * LANES)
+        here = [[value[:, lanes] for value in values] for values in terms]
+
+        def piece(start, count):
+            place = rows[start : start + count, lanes] - first[:, lanes]
+            return banded(jnp.bitwise_and(place, K - 1), here)
+
+        pieces = []
+        for m in range(CY):
+            line = [piece(m * N_GY + half * 16, 16)]
+            behind = piece(m * N_GY + (1 - half) * 16, 8) if m <= 2 else zeros
+            before = piece(m * N_GY + (1 - half) * 16 + 8, 8) if m == 7 else zeros
+            pieces += line + [behind, before] if half == 0 else [behind, before] + line
+        halves.append([jnp.concatenate([part[i] for part in pieces], axis=0) for i in range(2)])
+    return [jnp.concatenate([halves[0][i], halves[1][i]], axis=1) for i in range(2)]
+
+
 def spread_kernel(
     rows, charge, fraction, base_cell, live_slot, force_cot, potential_cot, hartley,
     send, spectral, atoms, table_a, table_b, table_c,
@@ -184,17 +210,10 @@
                 :, row * LANES : (row + 1) * LANES
             ]
 
-    def transformed(first, table):
-        value = split(product(hart, split(table)))
-        spectral[first] = value[0]
-        spectral[first + 1] = value[1]
-        return value
-
     cells = base_cell[0]
     slot = lax.broadcasted_iota(jnp.int32, (1, ATOMS), 1)
     base_z = jnp.bitwise_and(slot, -16) + jnp.bitwise_and(cells, 15)
-    place_z = jnp.bitwise_and(rows[...] - (base_z - 1), K - 1)
-    wz, dz = banded(place_z, spline_terms(fraction[2, 0]))
+    wz, dz = z_tables(rows, base_z - 1, spline_terms(fraction[2, 0]))
     tables = domain_tables(cells, fraction)
     for index, value in enumerate(tables):
         atoms[index * 16 : (index + 1) * 16, :] = value
@@ -213,10 +232,13 @@
         table_a[rows, :] = wx * (live_charge * wy)
         table_b[rows, :] = dx * (along_x * wy) + wx * (along_y * dy + direct * wy)
         table_c[rows, :] = wx * (along_z * wy)
-    hart = (hartley[0], hartley[1])
     nt = ((1,), (1,))
-    zw = transformed(0, wz)
-    zd = transformed(2, dz)
+    blocks = [(hartley[0, cut, :], hartley[1, cut, :]) for cut in HALVES]
+    zw, zd = [
+        joined([split(product(block, value)) for block in blocks]) for value in (split(wz), split(dz))
+    ]
+    for index, value in enumerate(zw + zd):
+        spectral[index] = value
     store(0, product(zw, split(table_a[...]), nt))
     store(1, product(zw, split(table_b[...]), nt) + product(zd, split(table_c[...]), nt))
 
@@ -273,18 +295,13 @@
     total_sq = jnp.transpose(square_y) + (square_x + square_z)
     factor = jnp.transpose(factor_y) * (factor_x * (factor_z * (1.0 / (math.pi * K))))
     kernel = jnp.where(total_sq > 0.0, factor / jnp.maximum(total_sq, 1.0), 0.0)
-    cuts = slice(0, K // 2), slice(K // 2, K)
-    hy = [(hartley[0, cut, :], hartley[1, cut, :]) for cut in cuts]
-
-    def joined(blocks):
-        return tuple(jnp.concatenate(pair, axis=0) for pair in zip(*blocks))
-
+    hy = [(hartley[0, cut, :], hartley[1, cut, :]) for cut in HALVES]
     lines = [
         jnp.concatenate([jnp.concatenate(group[m : m + 4], axis=0) for group in groups], axis=1)
         for m in (0, 4)
     ]
     half_way = joined([split(product(split(line), hx)) for line in lines])
-    spectrum = [product(block, half_way) * kernel[cut] for block, cut in zip(hy, cuts)]
+    spectrum = [product(block, half_way) * kernel[cut] for block, cut in zip(hy, HALVES)]
     spectrum = joined([split(block) for block in spectrum])
     half_way = [product(block, spectrum) for block in hy]
     solved = [product(split(block), hx) for block in half_way]

time: 80.6 us -> 80.5 us (level)
  no operation moved by 1% of the time
where the time goes in v7:
time: 80.5 us; the launch traced here: 80.3 us
  blocking collectives  75 us (93%)
  Pallas kernels  4.06 us (5%)
    all_to_all x2, blocking collectives, exchange(): lax.all_to_all(blocks.reshape(DEVICES, 2, LANES), ('gx', 'gy'), split_axi...  75 us
    pallas_call x1, Pallas kernels, on_device(): pl.pallas_call(plane_kernel, out_shape=message, in_specs=[vmem] * 4, out_...  1.83 us

profile of v7, /device:TPU:1, one launch (start us, length us, event | category | flops | bytes accessed | tf_op | source)
XLA Modules:
  0.0 80.3 jit_solution(10320942046027488350)
XLA Ops:
  0.7 0.0 copy-start.2
  0.7 0.0 copy-start.3
  0.7 0.0 copy-start.4
  0.7 0.0 copy-start.5
  0.7 0.0 copy-start.6
  0.7 0.0 copy-start.7
  0.7 0.3 tables.1.hartley
  1.0 0.3 copy-done.2
  1.4 0.0 copy-done.3
  1.4 0.0 copy-done.4
  1.4 0.0 copy-done.5
  1.4 0.0 copy-done.6
  1.4 0.0 copy-done.7
  1.4 0.8 %spread.1 = (f32[1024,128]{1,0:T(8,128)S(1)}, bf16[4,256,256]{2,1,0:T(8,128)(2,1)S(1)}, f32[264,256]{1,0:T(8,128)S(1)}) custom-call(s32[256,256]{1,0:T(8,128)S(1)} %rows.1, f32[1,1,256]{2,1,0:T(1,128)S(1)} %copy-done.4, f32[3,1,1,256]{3,2,1,0:T(1,128)S(1)} %copy-done.2, s32[1,1,256]{2,1,0:T(1,128)S(1)} %copy-done.5, s32[1,1,256]{2,1,0:T(1,128)S(1)} %copy-done.6, ...), custom_call_target="tpu_custom_call" | custom-call | tf_op jit(solution)/shard_map/spread/pallas_call | solution.py:407
  2.2 0.0 copy-start
  2.3 0.0 copy-start.1
  2.3 43.5 %all_to_all.10 = f32[512,2,128]{2,1,0:T(2,128)S(1)} all-to-all(f32[512,2,128]{2,1,0:T(2,128)S(1)} %bitcast.7), channel_id=1, replica_groups=mesh['gx'=16,'gy'=32] {'gx','gy'}, dimensions={0} | all-to-all | bytes 1048576 | tf_op jit(solution)/shard_map/all_to_all | solution.py:370
  45.8 0.0 copy-done
  45.8 0.0 copy-done.1
  45.8 1.8 %plane.1 = f32[1024,128]{1,0:T(8,128)S(1)} custom-call(f32[1024,128]{1,0:T(8,128)S(1)} %bitcast.4, bf16[2,256,256]{2,1,0:T(8,128)(2,1)S(1)} %tables.1.hartley, bf16[2,256,256]{2,1,0:T(8,128)(2,1)S(1)} %copy-done, f32[8,256]{1,0:T(8,128)S(1)} %copy-done.1), custom_call_target="tpu_custom_call" | custom-call | tf_op jit(solution)/shard_map/plane/pallas_call | solution.py:421
  47.6 31.5 %all_to_all.11 = f32[512,2,128]{2,1,0:T(2,128)S(1)} all-to-all(f32[512,2,128]{2,1,0:T(2,128)S(1)} %bitcast.5), channel_id=1, replica_groups=mesh['gx'=16,'gy'=32] {'gx','gy'}, dimensions={0} | all-to-all | bytes 1048576 | tf_op jit(solution)/shard_map/all_to_all | solution.py:370
  79.1 1.1 %sample.1 = (f32[3,1,1,256]{3,2,1,0:T(1,128)}, f32[1,1,256]{2,1,0:T(1,128)}, f32[1,1,256]{2,1,0:T(1,128)}) custom-call(f32[1024,128]{1,0:T(8,128)S(1)} %bitcast.6, bf16[4,256,256]{2,1,0:T(8,128)(2,1)S(1)} %get-tuple-element.7.spectral, f32[264,256]{1,0:T(8,128)S(1)} %get-tuple-element.8.atoms), custom_call_target="tpu_custom_call" | custom-call | tf_op jit(solution)/shard_map/sample/pallas_call | solution.py:430
  (1 shorter events, 0.0 us)
Async XLA Ops:
  0.7 0.7 copy-start.2
  0.7 0.7 copy-start.3
  0.7 0.7 copy-start.4
  0.7 0.7 copy-start.5
  0.7 0.7 copy-start.6
  0.7 0.7 copy-start.7
  2.2 43.5 %copy-start = (bf16[2,256,256]{2,1,0:T(8,128)(2,1)S(1)}, bf16[2,256,256]{2,1,0:T(8,128)(2,1)}, u32[]{:S(2)}) copy-start(bf16[2,256,256]{2,1,0:T(8,128)(2,1)} %constant.4.clone.hartley_x) | copy-start | bytes 786436
  2.3 43.5 %copy-start.1 = (f32[8,256]{1,0:T(8,128)S(1)}, f32[8,256]{1,0:T(8,128)}, u32[]{:S(2)}) copy-start(f32[8,256]{1,0:T(8,128)} %constant.5.clone.terms) | copy-start | bytes 24580

commit v8 on v7

--- a/solution.py
+++ b/solution.py
@@ -243,16 +243,20 @@
     store(1, product(zw, split(table_b[...]), nt) + product(zd, split(table_c[...]), nt))
 
 
-def transposed_blocks(values):
-    values = list(values)
-    block = jnp.right_shift(lax.broadcasted_iota(jnp.int32, values[0].shape, 1), 4)
-    for step in (1, 2, 4):
+def exchanged(values, steps, members):
+    block = jnp.right_shift(lax.broadcasted_iota(jnp.int32, values[members[0]].shape, 1), 4)
+    for step in steps:
         upper = jnp.bitwise_and(block, step) != 0
-        for i in range(8):
+        for i in members:
             if i & step == 0:
                 first, second = values[i], values[i + step]
                 values[i] = jnp.where(upper, pltpu.roll(second, 16 * step, 1), first)
                 values[i + step] = jnp.where(upper, second, pltpu.roll(first, LANES - 16 * step, 1))
+
+
+def transposed_blocks(values):
+    values = list(values)
+    exchanged(values, (1, 2, 4), range(8))
     return values
 
 
@@ -291,16 +295,21 @@
         side = received[rows(gx, 1), :] + from_sides(corners, gx)
         after, before = pltpu.roll(side, N_GY - 1, 0), pltpu.roll(side, 1, 0)
         folded.append(own + jnp.where(last, after, jnp.where(first, before, 0.0)))
-    groups = [transposed_blocks(folded[group * 8 : group * 8 + 8]) for group in range(2)]
     total_sq = jnp.transpose(square_y) + (square_x + square_z)
     factor = jnp.transpose(factor_y) * (factor_x * (factor_z * (1.0 / (math.pi * K))))
     kernel = jnp.where(total_sq > 0.0, factor / jnp.maximum(total_sq, 1.0), 0.0)
     hy = [(hartley[0, cut, :], hartley[1, cut, :]) for cut in HALVES]
-    lines = [
-        jnp.concatenate([jnp.concatenate(group[m : m + 4], axis=0) for group in groups], axis=1)
-        for m in (0, 4)
-    ]
-    half_way = joined([split(product(split(line), hx)) for line in lines])
+    groups = [folded[0:8], folded[8:16]]
+    for group in groups:
+        exchanged(group, (4,), range(8))
+    lines = []
+    for low_line in (0, 4):
+        members = range(low_line, low_line + 4)
+        for group in groups:
+            exchanged(group, (2, 1), members)
+        line = [jnp.concatenate([group[m] for m in members], axis=0) for group in groups]
+        lines.append(split(product(split(jnp.concatenate(line, axis=1)), hx)))
+    half_way = joined(lines)
     spectrum = [product(block, half_way) * kernel[cut] for block, cut in zip(hy, HALVES)]
     spectrum = joined([split(block) for block in spectrum])
     half_way = [product(block, spectrum) for block in hy]

time: 80.5 us -> 80.5 us (level)
  no operation moved by 1% of the time
where the time goes in v8:
time: 80.5 us; the launch traced here: 80.3 us
  blocking collectives  75 us (93%)
  Pallas kernels  4.07 us (5%)
    all_to_all x2, blocking collectives, exchange(): lax.all_to_all(blocks.reshape(DEVICES, 2, LANES), ('gx', 'gy'), split_axi...  75 us
    pallas_call x1, Pallas kernels, on_device(): pl.pallas_call(plane_kernel, out_shape=message, in_specs=[vmem] * 4, out_...  1.83 us

profile of v8, /device:TPU:1, one launch (start us, length us, event | category | flops | bytes accessed | tf_op | source)
XLA Modules:
  0.0 80.3 jit_solution(12347294815949087782)
XLA Ops:
  0.7 0.0 copy-start.2
  0.7 0.0 copy-start.3
  0.7 0.0 copy-start.4
  0.7 0.0 copy-start.5
  0.7 0.0 copy-start.6
  0.7 0.0 copy-start.7
  0.7 0.3 tables.1.hartley
  1.0 0.3 copy-done.2
  1.4 0.0 copy-done.3
  1.4 0.0 copy-done.4
  1.4 0.0 copy-done.5
  1.4 0.0 copy-done.6
  1.4 0.0 copy-done.7
  1.4 0.8 %spread.1 = (f32[1024,128]{1,0:T(8,128)S(1)}, bf16[4,256,256]{2,1,0:T(8,128)(2,1)S(1)}, f32[264,256]{1,0:T(8,128)S(1)}) custom-call(s32[256,256]{1,0:T(8,128)S(1)} %rows.1, f32[1,1,256]{2,1,0:T(1,128)S(1)} %copy-done.4, f32[3,1,1,256]{3,2,1,0:T(1,128)S(1)} %copy-done.2, s32[1,1,256]{2,1,0:T(1,128)S(1)} %copy-done.5, s32[1,1,256]{2,1,0:T(1,128)S(1)} %copy-done.6, ...), custom_call_target="tpu_custom_call" | custom-call | tf_op jit(solution)/shard_map/spread/pallas_call | solution.py:416
  2.2 0.0 copy-start
  2.3 0.0 copy-start.1
  2.3 43.5 %all_to_all.10 = f32[512,2,128]{2,1,0:T(2,128)S(1)} all-to-all(f32[512,2,128]{2,1,0:T(2,128)S(1)} %bitcast.7), channel_id=1, replica_groups=mesh['gx'=16,'gy'=32] {'gx','gy'}, dimensions={0} | all-to-all | bytes 1048576 | tf_op jit(solution)/shard_map/all_to_all | solution.py:379
  45.8 0.0 copy-done
  45.8 0.0 copy-done.1
  45.8 1.8 %plane.1 = f32[1024,128]{1,0:T(8,128)S(1)} custom-call(f32[1024,128]{1,0:T(8,128)S(1)} %bitcast.4, bf16[2,256,256]{2,1,0:T(8,128)(2,1)S(1)} %tables.1.hartley, bf16[2,256,256]{2,1,0:T(8,128)(2,1)S(1)} %copy-done, f32[8,256]{1,0:T(8,128)S(1)} %copy-done.1), custom_call_target="tpu_custom_call" | custom-call | tf_op jit(solution)/shard_map/plane/pallas_call | solution.py:430
  47.6 31.5 %all_to_all.11 = f32[512,2,128]{2,1,0:T(2,128)S(1)} all-to-all(f32[512,2,128]{2,1,0:T(2,128)S(1)} %bitcast.5), channel_id=1, replica_groups=mesh['gx'=16,'gy'=32] {'gx','gy'}, dimensions={0} | all-to-all | bytes 1048576 | tf_op jit(solution)/shard_map/all_to_all | solution.py:379
  79.1 1.1 %sample.1 = (f32[3,1,1,256]{3,2,1,0:T(1,128)}, f32[1,1,256]{2,1,0:T(1,128)}, f32[1,1,256]{2,1,0:T(1,128)}) custom-call(f32[1024,128]{1,0:T(8,128)S(1)} %bitcast.6, bf16[4,256,256]{2,1,0:T(8,128)(2,1)S(1)} %get-tuple-element.7.spectral, f32[264,256]{1,0:T(8,128)S(1)} %get-tuple-element.8.atoms), custom_call_target="tpu_custom_call" | custom-call | tf_op jit(solution)/shard_map/sample/pallas_call | solution.py:439
  (1 shorter events, 0.0 us)
Async XLA Ops:
  0.7 0.7 copy-start.2
  0.7 0.7 copy-start.3
  0.7 0.7 copy-start.4
  0.7 0.7 copy-start.5
  0.7 0.7 copy-start.6
  0.7 0.7 copy-start.7
  2.2 43.5 %copy-start = (bf16[2,256,256]{2,1,0:T(8,128)(2,1)S(1)}, bf16[2,256,256]{2,1,0:T(8,128)(2,1)}, u32[]{:S(2)}) copy-start(bf16[2,256,256]{2,1,0:T(8,128)(2,1)} %constant.4.clone.hartley_x) | copy-start | bytes 786436
  2.3 43.5 %copy-start.1 = (f32[8,256]{1,0:T(8,128)S(1)}, f32[8,256]{1,0:T(8,128)}, u32[]{:S(2)}) copy-start(f32[8,256]{1,0:T(8,128)} %constant.5.clone.terms) | copy-start | bytes 24580

commit v9 on v7

--- a/solution.py
+++ b/solution.py
@@ -330,7 +330,7 @@
 
 
 def sample_kernel(
-    received, spectral, atoms, forces, potential, charge_grad, sample_a, sample_b, sample_c
+    received, spectral, atoms, forces, potential, charge_grad
 ):
     def field(index):
         halves = [received[pl.ds(index * 2 * K + half, K, stride=2), :] for half in range(2)]
@@ -339,9 +339,7 @@
     zw = (spectral[0], spectral[1])
     zd = (spectral[2], spectral[3])
     first = field(0)
-    sample_a[...] = product(first, zw)
-    sample_b[...] = product(first, zd)
-    sample_c[...] = product(field(1), zw)
+    along, sloped, answered = product(first, zw), product(first, zd), product(field(1), zw)
     live, live_charge, along_x, along_y, along_z = [
         atoms[SCALARS + row : SCALARS + row + 1, :] for row in range(5)
     ]
@@ -349,13 +347,13 @@
     sums = [jnp.zeros((16, ATOMS), jnp.float32) for _ in range(5)]
     for index, (wx, dx, wy, dy) in enumerate(message_blocks(tables)):
         rows = slice(index * 16, (index + 1) * 16)
-        plain = sample_a[rows, :]
+        plain = along[rows, :]
         plain_x = wx * plain
         sums[0] = sums[0] + plain_x * wy
         sums[1] = sums[1] + (dx * plain) * wy
         sums[2] = sums[2] + plain_x * dy
-        sums[3] = sums[3] + (wx * sample_b[rows, :]) * wy
-        sums[4] = sums[4] + (wx * sample_c[rows, :]) * wy
+        sums[3] = sums[3] + (wx * sloped[rows, :]) * wy
+        sums[4] = sums[4] + (wx * answered[rows, :]) * wy
     mesh_value, grad_x, grad_y, grad_z, response = [
         jnp.sum(value, axis=0, keepdims=True) for value in sums
     ]
@@ -436,7 +434,6 @@
         ),
         in_specs=[vmem] * 3,
         out_specs=(vmem, vmem, vmem),
-        scratch_shapes=[table, table, table],
         compiler_params=params,
         name="sample",
     )(returned, spectral, atoms)

time: 80.5 us -> 80.5 us (level)
  no operation moved by 1% of the time
where the time goes in v9:
time: 80.5 us; the launch traced here: 80.3 us
  blocking collectives  75 us (93%)
  Pallas kernels  4.06 us (5%)
    all_to_all x2, blocking collectives, exchange(): lax.all_to_all(blocks.reshape(DEVICES, 2, LANES), ('gx', 'gy'), split_axi...  75 us
    pallas_call x1, Pallas kernels, on_device(): pl.pallas_call(plane_kernel, out_shape=message, in_specs=[vmem] * 4, out_...  1.83 us

profile of v9, /device:TPU:1, one launch (start us, length us, event | category | flops | bytes accessed | tf_op | source)
XLA Modules:
  0.0 80.3 jit_solution(10320942046027488350)
XLA Ops:
  0.7 0.0 copy-start.2
  0.7 0.0 copy-start.3
  0.7 0.0 copy-start.4
  0.7 0.0 copy-start.5
  0.7 0.0 copy-start.6
  0.7 0.0 copy-start.7
  0.7 0.3 tables.1.hartley
  1.0 0.3 copy-done.2
  1.4 0.0 copy-done.3
  1.4 0.0 copy-done.4
  1.4 0.0 copy-done.5
  1.4 0.0 copy-done.6
  1.4 0.0 copy-done.7
  1.4 0.8 %spread.1 = (f32[1024,128]{1,0:T(8,128)S(1)}, bf16[4,256,256]{2,1,0:T(8,128)(2,1)S(1)}, f32[264,256]{1,0:T(8,128)S(1)}) custom-call(s32[256,256]{1,0:T(8,128)S(1)} %rows.1, f32[1,1,256]{2,1,0:T(1,128)S(1)} %copy-done.4, f32[3,1,1,256]{3,2,1,0:T(1,128)S(1)} %copy-done.2, s32[1,1,256]{2,1,0:T(1,128)S(1)} %copy-done.5, s32[1,1,256]{2,1,0:T(1,128)S(1)} %copy-done.6, ...), custom_call_target="tpu_custom_call" | custom-call | tf_op jit(solution)/shard_map/spread/pallas_call | solution.py:405
  2.2 0.0 copy-start
  2.3 0.0 copy-start.1
  2.3 43.5 %all_to_all.10 = f32[512,2,128]{2,1,0:T(2,128)S(1)} all-to-all(f32[512,2,128]{2,1,0:T(2,128)S(1)} %bitcast.7), channel_id=1, replica_groups=mesh['gx'=16,'gy'=32] {'gx','gy'}, dimensions={0} | all-to-all | bytes 1048576 | tf_op jit(solution)/shard_map/all_to_all | solution.py:368
  45.8 0.0 copy-done
  45.8 0.0 copy-done.1
  45.8 1.8 %plane.1 = f32[1024,128]{1,0:T(8,128)S(1)} custom-call(f32[1024,128]{1,0:T(8,128)S(1)} %bitcast.4, bf16[2,256,256]{2,1,0:T(8,128)(2,1)S(1)} %tables.1.hartley, bf16[2,256,256]{2,1,0:T(8,128)(2,1)S(1)} %copy-done, f32[8,256]{1,0:T(8,128)S(1)} %copy-done.1), custom_call_target="tpu_custom_call" | custom-call | tf_op jit(solution)/shard_map/plane/pallas_call | solution.py:419
  47.6 31.5 %all_to_all.11 = f32[512,2,128]{2,1,0:T(2,128)S(1)} all-to-all(f32[512,2,128]{2,1,0:T(2,128)S(1)} %bitcast.5), channel_id=1, replica_groups=mesh['gx'=16,'gy'=32] {'gx','gy'}, dimensions={0} | all-to-all | bytes 1048576 | tf_op jit(solution)/shard_map/all_to_all | solution.py:368
  79.1 1.1 %sample.1 = (f32[3,1,1,256]{3,2,1,0:T(1,128)}, f32[1,1,256]{2,1,0:T(1,128)}, f32[1,1,256]{2,1,0:T(1,128)}) custom-call(f32[1024,128]{1,0:T(8,128)S(1)} %bitcast.6, bf16[4,256,256]{2,1,0:T(8,128)(2,1)S(1)} %get-tuple-element.7.spectral, f32[264,256]{1,0:T(8,128)S(1)} %get-tuple-element.8.atoms), custom_call_target="tpu_custom_call" | custom-call | tf_op jit(solution)/shard_map/sample/pallas_call | solution.py:428
  (1 shorter events, 0.0 us)
Async XLA Ops:
  0.7 0.7 copy-start.2
  0.7 0.7 copy-start.3
  0.7 0.7 copy-start.4
  0.7 0.7 copy-start.5
  0.7 0.7 copy-start.6
  0.7 0.7 copy-start.7
  2.2 43.5 %copy-start = (bf16[2,256,256]{2,1,0:T(8,128)(2,1)S(1)}, bf16[2,256,256]{2,1,0:T(8,128)(2,1)}, u32[]{:S(2)}) copy-start(bf16[2,256,256]{2,1,0:T(8,128)(2,1)} %constant.4.clone.hartley_x) | copy-start | bytes 786436
  2.3 43.5 %copy-start.1 = (f32[8,256]{1,0:T(8,128)S(1)}, f32[8,256]{1,0:T(8,128)}, u32[]{:S(2)}) copy-start(f32[8,256]{1,0:T(8,128)} %constant.5.clone.terms) | copy-start | bytes 24580

commit v10 on v8

--- a/solution.py
+++ b/solution.py
@@ -132,16 +132,16 @@
     return out
 
 
-def domain_tables(cells, fraction_ref):
+def domain_tables(cells, fraction_ref, rows):
     cell_x = jnp.right_shift(cells, 7) - 1
     cell_y = jnp.bitwise_and(jnp.right_shift(cells, 4), CY - 1) - 1
     terms_x = spline_terms(fraction_ref[0, 0])
     terms_y = spline_terms(fraction_ref[1, 0])
     lane = row_numbers(16)
-    out = banded(lane - cell_x, terms_x) + banded(halo_x(lane) - cell_x, terms_x)
+    out = banded(lane - cell_x, terms_x) + banded(rows[K : K + 16, :] - cell_x, terms_x)
     out += banded(lane - 1 - cell_y, terms_y)
     for j in range(2, 7):
-        out += banded(halo_y(lane, j) - cell_y, terms_y)
+        out += banded(rows[K + 16 * j - 16 : K + 16 * j, :] - cell_y, terms_y)
     return out
 
 
@@ -161,11 +161,15 @@
 
 
 def rows_kernel(rows):
-    rows[...] = natural(row_numbers(K))
+    rows[0:K, :] = natural(row_numbers(K))
+    lane = row_numbers(16)
+    rows[K : K + 16, :] = halo_x(lane)
+    for j in range(2, 7):
+        rows[K + 16 * j - 16 : K + 16 * j, :] = halo_y(lane, j)
 
 
 def table_kernel(rows, hartley):
-    cell = rows[...]
+    cell = rows[0:K, :]
     frequency = natural(lax.broadcasted_iota(jnp.int32, (K, K), 1))
     turn = jnp.bitwise_and(cell * frequency + K // 8, K - 1) - K // 2
     quarter = jnp.where(turn > K // 4, K // 2 - turn, jnp.where(turn < -K // 4, -K // 2 - turn, turn))
@@ -214,7 +218,7 @@
     slot = lax.broadcasted_iota(jnp.int32, (1, ATOMS), 1)
     base_z = jnp.bitwise_and(slot, -16) + jnp.bitwise_and(cells, 15)
     wz, dz = z_tables(rows, base_z - 1, spline_terms(fraction[2, 0]))
-    tables = domain_tables(cells, fraction)
+    tables = domain_tables(cells, fraction, rows)
     for index, value in enumerate(tables):
         atoms[index * 16 : (index + 1) * 16, :] = value
     live = live_slot[0].astype(jnp.float32)
@@ -398,7 +402,7 @@
 
     rows = pl.pallas_call(
         rows_kernel,
-        out_shape=jax.ShapeDtypeStruct((K, ATOMS), jnp.int32),
+        out_shape=jax.ShapeDtypeStruct((K + 96, ATOMS), jnp.int32),
         out_specs=vmem,
         compiler_params=params,
         cost_estimate=pl.CostEstimate(flops=10**9, bytes_accessed=10**6, transcendentals=0),

time: 80.5 us -> 80.5 us (level)
  no operation moved by 1% of the time
where the time goes in v10:
time: 80.5 us; the launch traced here: 80.3 us
  blocking collectives  75 us (93%)
  Pallas kernels  4.07 us (5%)
    all_to_all x2, blocking collectives, exchange(): lax.all_to_all(blocks.reshape(DEVICES, 2, LANES), ('gx', 'gy'), split_axi...  75 us
    pallas_call x1, Pallas kernels, on_device(): pl.pallas_call(plane_kernel, out_shape=message, in_specs=[vmem] * 4, out_...  1.84 us

profile of v10, /device:TPU:1, one launch (start us, length us, event | category | flops | bytes accessed | tf_op | source)
XLA Modules:
  0.0 80.3 jit_solution(9197500725778227503)
XLA Ops:
  0.7 0.0 copy-start.2
  0.7 0.0 copy-start.3
  0.7 0.0 copy-start.4
  0.7 0.0 copy-start.5
  0.7 0.0 copy-start.6
  0.7 0.0 copy-start.7
  0.7 0.3 tables.1.hartley
  1.0 0.3 copy-done.2
  1.4 0.0 copy-done.3
  1.4 0.0 copy-done.4
  1.4 0.0 copy-done.5
  1.4 0.0 copy-done.6
  1.4 0.0 copy-done.7
  1.4 0.8 %spread.1 = (f32[1024,128]{1,0:T(8,128)S(1)}, bf16[4,256,256]{2,1,0:T(8,128)(2,1)S(1)}, f32[264,256]{1,0:T(8,128)S(1)}) custom-call(s32[352,256]{1,0:T(8,128)S(1)} %rows.1, f32[1,1,256]{2,1,0:T(1,128)S(1)} %copy-done.4, f32[3,1,1,256]{3,2,1,0:T(1,128)S(1)} %copy-done.2, s32[1,1,256]{2,1,0:T(1,128)S(1)} %copy-done.5, s32[1,1,256]{2,1,0:T(1,128)S(1)} %copy-done.6, ...), custom_call_target="tpu_custom_call" | custom-call | tf_op jit(solution)/shard_map/spread/pallas_call | solution.py:420
  2.2 0.0 copy-start
  2.3 0.0 copy-start.1
  2.3 43.5 %all_to_all.10 = f32[512,2,128]{2,1,0:T(2,128)S(1)} all-to-all(f32[512,2,128]{2,1,0:T(2,128)S(1)} %bitcast.7), channel_id=1, replica_groups=mesh['gx'=16,'gy'=32] {'gx','gy'}, dimensions={0} | all-to-all | bytes 1048576 | tf_op jit(solution)/shard_map/all_to_all | solution.py:383
  45.8 0.0 copy-done
  45.8 0.0 copy-done.1
  45.8 1.8 %plane.1 = f32[1024,128]{1,0:T(8,128)S(1)} custom-call(f32[1024,128]{1,0:T(8,128)S(1)} %bitcast.4, bf16[2,256,256]{2,1,0:T(8,128)(2,1)S(1)} %tables.1.hartley, bf16[2,256,256]{2,1,0:T(8,128)(2,1)S(1)} %copy-done, f32[8,256]{1,0:T(8,128)S(1)} %copy-done.1), custom_call_target="tpu_custom_call" | custom-call | tf_op jit(solution)/shard_map/plane/pallas_call | solution.py:434
  47.6 31.5 %all_to_all.11 = f32[512,2,128]{2,1,0:T(2,128)S(1)} all-to-all(f32[512,2,128]{2,1,0:T(2,128)S(1)} %bitcast.5), channel_id=1, replica_groups=mesh['gx'=16,'gy'=32] {'gx','gy'}, dimensions={0} | all-to-all | bytes 1048576 | tf_op jit(solution)/shard_map/all_to_all | solution.py:383
  79.1 1.1 %sample.1 = (f32[3,1,1,256]{3,2,1,0:T(1,128)}, f32[1,1,256]{2,1,0:T(1,128)}, f32[1,1,256]{2,1,0:T(1,128)}) custom-call(f32[1024,128]{1,0:T(8,128)S(1)} %bitcast.6, bf16[4,256,256]{2,1,0:T(8,128)(2,1)S(1)} %get-tuple-element.7.spectral, f32[264,256]{1,0:T(8,128)S(1)} %get-tuple-element.8.atoms), custom_call_target="tpu_custom_call" | custom-call | tf_op jit(solution)/shard_map/sample/pallas_call | solution.py:443
  (1 shorter events, 0.0 us)
Async XLA Ops:
  0.7 0.7 copy-start.2
  0.7 0.7 copy-start.3
  0.7 0.7 copy-start.4
  0.7 0.7 copy-start.5
  0.7 0.7 copy-start.6
  0.7 0.7 copy-start.7
  2.2 43.5 %copy-start = (bf16[2,256,256]{2,1,0:T(8,128)(2,1)S(1)}, bf16[2,256,256]{2,1,0:T(8,128)(2,1)}, u32[]{:S(2)}) copy-start(bf16[2,256,256]{2,1,0:T(8,128)(2,1)} %constant.4.clone.hartley_x) | copy-start | bytes 786436
  2.3 43.5 %copy-start.1 = (f32[8,256]{1,0:T(8,128)S(1)}, f32[8,256]{1,0:T(8,128)}, u32[]{:S(2)}) copy-start(f32[8,256]{1,0:T(8,128)} %constant.5.clone.terms) | copy-start | bytes 24580
